TPU v7x, 32 devices: a whole 2x2x4 slice. The times are simulated.
32 devices in a mesh: head: 4 (over z), ctx: 8 (over y, x, core).
Axes of the slice: x: 2, y: 2, z: 4, core: 2. Of those that a mesh axis runs over, the one named last changes fastest.
Arguments:
- inputs: bfloat16 [2048, 4096], P('ctx'), may hold values from -8 to 8
- out_grad: bfloat16 [2048, 4096], P('ctx', 'head'), may hold values from -6 to 6
- w_query: bfloat16 [4096, 4096], P(None, 'head'), may hold values from -4 to 4
- w_key: bfloat16 [4096, 1024], P(None, 'head'), may hold values from -4 to 4
- value_projection: bfloat16 [4096, 1024], P(None, 'head'), may hold values from -0.09375 to 0.09375
- w_out: bfloat16 [4096, 4096], P('head'), may hold values from -0.09375 to 0.09375
- doc_lengths: int32 [8], replicated, may hold values from 1 to 1024, 2048 in all
- span_order: int32 [16], replicated, may hold values from 0 to 15, as said below
Outputs:
- input_grad: bfloat16 [2048, 4096], P('ctx', 'head')
Inputs may be any that keep to these rules, and one draw needn't show every extreme that they name: `span_order`: A permutation of 0 to 15; entries 2 d and 2 d + 1 are c and 15 - c for some c, in either order.
All inputs are finite; a program needn't handle non-finite values.
Results may differ from a plain program's by a relative error of at most 0.012.
The roundings to bfloat16 on the way count: a program that leaves them out, or rounds other values in their place, can miss the bound.
Values may be sent and summed in bfloat16 or wider, within the bound.
No kernel may reach another device: no remote copies, remote signals or barrier semaphores. Data moves between devices by JAX's collectives and lax.ppermute only.
A program may use at most 64 MiB of HBM per device.

v0:
```python
import math

import jax
import jax.numpy as jnp
from jax import lax
from jax.sharding import PartitionSpec as P

ASKER_NUM = 32
SHARED_KV_NUM = 8
CHANNEL_DIM = 128


masked_score = -1e30


def doc_index(positions, doc_lengths):
    ends = jnp.cumsum(doc_lengths)
    return jnp.sum((positions[:, None] >= ends[None, :]).astype(jnp.int32), axis=1)


def block_scores(query_part, key_part, query_pos, query_docs, key_pos, key_docs):
    scale = 1.0 / math.sqrt(CHANNEL_DIM)
    logits = (
        jnp.einsum("qagd,kad->agqk", query_part, key_part, preferred_element_type=jnp.float32)
        * scale
    )
    allowed = (key_pos[None, :] <= query_pos[:, None]) & (key_docs[None, :] == query_docs[:, None])
    return (jnp.where(allowed[None, None], logits, masked_score), allowed)


def back_project(grad, weight):
    return lax.dot_general(
        grad, weight, (((1,), (1,)), ((), ())), preferred_element_type=jnp.float32
    )


def stream_stats(
    query_heads,
    grad_heads,
    own_positions,
    own_documents,
    key_blocks,
    value_blocks,
    position_blocks,
    document_blocks,
    kv_heads,
    sharing_bundles,
    tokens,
):

    def gather_stats(carry, item):
        maxima, totals, inner = carry
        key_part, value_part, key_pos, key_docs = item
        logits, allowed = block_scores(
            query_heads, key_part, own_positions, own_documents, key_pos, key_docs
        )
        fresh = jnp.maximum(maxima, jnp.max(logits, axis=3))
        factor = jnp.exp(maxima - fresh)
        weights = jnp.where(allowed[None, None], jnp.exp(logits - fresh[..., None]), 0.0)
        slopes = jnp.einsum(
            "qagd,kad->agqk", grad_heads, value_part, preferred_element_type=jnp.float32
        )
        totals = totals * factor + jnp.sum(weights, axis=3)
        inner = inner * factor + jnp.sum(weights * slopes, axis=3)
        return ((fresh, totals, inner), 0)

    start_max = jnp.full((kv_heads, sharing_bundles, tokens), masked_score, jnp.float32)
    start_sum = jnp.zeros((kv_heads, sharing_bundles, tokens), jnp.float32)
    (maxima, totals, inner), unused = lax.scan(
        gather_stats,
        (start_max, start_sum, start_sum),
        (key_blocks, value_blocks, position_blocks, document_blocks),
    )
    return (maxima, totals, inner / totals)


def shards(inputs, out_grad, w_query, w_key, value_projection, w_out, doc_lengths, span_order):
    tokens = inputs.shape[0]
    half = tokens // 2
    length = span_order.shape[0] * half
    kv_heads = w_key.shape[1] // CHANNEL_DIM
    sharing_bundles = ASKER_NUM // SHARED_KV_NUM
    width = w_key.shape[1]
    scale = 1.0 / math.sqrt(CHANNEL_DIM)
    block = math.gcd(length, 512)
    count = length // block
    offsets = jnp.arange(half, dtype=jnp.int32)
    all_positions = (span_order[:, None] * half + offsets[None, :]).reshape(length)
    all_documents = doc_index(all_positions, doc_lengths)
    mine = lax.axis_index("ctx")
    own_positions = lax.dynamic_slice_in_dim(all_positions, mine * tokens, tokens)
    own_documents = lax.dynamic_slice_in_dim(all_documents, mine * tokens, tokens)
    position_blocks = all_positions.reshape(count, block)
    document_blocks = all_documents.reshape(count, block)
    query = jnp.dot(inputs, w_query, preferred_element_type=jnp.float32).astype(jnp.bfloat16)
    keys = jnp.dot(inputs, w_key, preferred_element_type=jnp.float32).astype(jnp.bfloat16)
    values = jnp.dot(inputs, value_projection, preferred_element_type=jnp.float32).astype(
        jnp.bfloat16
    )
    columns = w_out
    context_grad = back_project(
        lax.all_gather(out_grad, "head", axis=1, tiled=True), columns
    ).astype(jnp.bfloat16)
    gathered = lax.all_gather(jnp.concatenate([keys, values], axis=1), "ctx", axis=0, tiled=True)
    paired = gathered.reshape(count, block, 2, kv_heads, CHANNEL_DIM)
    key_blocks = paired[:, :, 0]
    value_blocks = paired[:, :, 1]
    query_heads = query.reshape(tokens, kv_heads, sharing_bundles, CHANNEL_DIM)
    grad_heads = context_grad.reshape(tokens, kv_heads, sharing_bundles, CHANNEL_DIM)
    maxima, totals, delta = stream_stats(
        query_heads,
        grad_heads,
        own_positions,
        own_documents,
        key_blocks,
        value_blocks,
        position_blocks,
        document_blocks,
        kv_heads,
        sharing_bundles,
        tokens,
    )

    def key_side(query_acc, item):
        key_part, value_part, key_pos, key_docs = item
        logits, allowed = block_scores(
            query_heads, key_part, own_positions, own_documents, key_pos, key_docs
        )
        probability = jnp.where(
            allowed[None, None], jnp.exp(logits - maxima[..., None]) / totals[..., None], 0.0
        )
        slopes = jnp.einsum(
            "qagd,kad->agqk", grad_heads, value_part, preferred_element_type=jnp.float32
        )
        score_grad = (probability * (slopes - delta[..., None])).astype(jnp.bfloat16)
        rounded = probability.astype(jnp.bfloat16)
        value_term = jnp.einsum(
            "agqk,qagd->kad", rounded, grad_heads, preferred_element_type=jnp.float32
        )
        key_term = (
            jnp.einsum(
                "agqk,qagd->kad", score_grad, query_heads, preferred_element_type=jnp.float32
            )
            * scale
        )
        query_acc = query_acc + jnp.einsum(
            "agqk,kad->qagd", score_grad, key_part, preferred_element_type=jnp.float32
        )
        return (
            query_acc,
            jnp.concatenate([key_term.reshape(block, -1), value_term.reshape(block, -1)], axis=1),
        )

    query_acc, lookup_pieces = lax.scan(
        key_side,
        jnp.zeros((tokens, kv_heads, sharing_bundles, CHANNEL_DIM), jnp.float32),
        (key_blocks, value_blocks, position_blocks, document_blocks),
    )
    query_grad = (query_acc * scale).reshape(tokens, -1).astype(jnp.bfloat16)
    owned = lax.psum_scatter(
        lookup_pieces.reshape(length, -1), "ctx", scatter_dimension=0, tiled=True
    ).astype(jnp.bfloat16)
    key_gradient = owned[:, :width]
    value_gradient = owned[:, width:]
    partial_value = (
        back_project(query_grad, w_query)
        + back_project(key_gradient, w_key)
        + back_project(value_gradient, value_projection)
    )
    summed = lax.psum(partial_value, "head")
    columns = partial_value.shape[1] // lax.axis_size("head")
    return lax.dynamic_slice_in_dim(summed, lax.axis_index("head") * columns, columns, 1).astype(
        jnp.bfloat16
    )


def solution(mesh):
    in_specs = (
        P("ctx", None),
        P("ctx", "head"),
        P(None, "head"),
        P(None, "head"),
        P(None, "head"),
        P("head", None),
        P(),
        P(),
    )
    out_specs = P("ctx", "head")
    return jax.shard_map(shards, mesh=mesh, in_specs=in_specs, out_specs=out_specs, check_vma=False)
```

profile of v0, /device:TPU:0, one launch (start us, length us, event | category | flops | bytes accessed | tf_op | source)
XLA Modules:
  0.0 394.6 jit_solution(17151706125546352946)
XLA Ops:
  8.1 2.7 convolution_convert_fusion.3
  13.4 6.3 %convolution_convert_fusion.1 = bf16[256,1024]{1,0:T(8,128)(2,1)S(1)} fusion(bf16[256,4096]{1,0:T(8,128)(2,1)} %param.12, bf16[4096,1024]{1,0:T(8,128)(2,1)} %param.14), kind=kOutput, calls=%fused_computation.53 | convolution fusion | flops 2147745792 | bytes 11010048 | tf_op jit(solution)/shard_map/dot_general | solution.py:95
  21.4 36.2 %all-gather.5.cloned.1.call-done = bf16[256,4096]{1,0:T(8,128)(2,1)} async-done(((bf16[256,1024]{1,0:T(8,128)(2,1)}), bf16[256,4096]{1,0:T(8,128)(2,1)}) %all-gather.5.cloned.1.call-update) | async-done | bytes 2097168 | tf_op jit(solution)/shard_map/all_gather | solution.py:102
  57.6 7.2 %convolution_convert_fusion = bf16[256,1024]{1,0:T(8,128)(2,1)} fusion(bf16[256,4096]{1,0:T(8,128)(2,1)} %all-gather.5.cloned.1.call-done, bf16[1024,4096]{1,0:T(8,128)(2,1)} %param.17), kind=kOutput, calls=%fused_computation.52 | convolution fusion | flops 2147745792 | bytes 11010048 | tf_op jit(solution)/shard_map/dot_general | solution.py:32
  68.2 18.2 %all-gather.3.cloned.1.call-done = bf16[2048,512]{0,1:T(8,128)(2,1)} async-done(((bf16[256,512]{0,1:T(8,128)(2,1)}), bf16[2048,512]{0,1:T(8,128)(2,1)}) %all-gather.3.cloned.1.call-update) | async-done | bytes 2097168 | tf_op jit(solution)/shard_map/all_gather | solution.py:104
  86.4 4.5 %reshape.188 = bf16[4,512,2,2,128]{1,0,4,3,2:T(4,128)(2,1)} reshape(bf16[2048,512]{0,1:T(8,128)(2,1)} %all-gather.3.cloned.1.call-done) | data formatting | bytes 4194304 | tf_op jit(solution)/shard_map/reshape | solution.py:105
  91.0 3.7 fusion.33
  94.6 2.6 copy.64
  97.3 2.6 copy.63
  99.9 21.7 %while.28 = (s32[]{:T(128)}, f32[2,4,256]{2,1,0:T(4,128)S(1)}, f32[2,4,256]{2,1,0:T(4,128)S(1)}, f32[2,4,256]{2,1,0:T(4,128)S(1)}, s32[4,512]{1,0:T(4,128)S(1)},...) while((s32[]{:T(128)}, f32[2,4,256]{2,1,0:T(4,128)S(1)}, ...), condition=%wide.region_6.7_spmd.clone, body=%wide.region_2.6_spmd.clone.sunk | while | flops 551958528 | bytes 14842020 | solution.py:69
  100.1 1.7 fusion.80
  101.9 2.4 fusion.81
  105.6 1.7 fusion.80
  107.3 2.4 fusion.81
  111.0 1.7 fusion.80
  112.8 2.4 fusion.81
  116.5 1.7 fusion.80
  118.2 2.4 fusion.81
  121.7 58.8 %while.29 = (s32[]{:T(128)}, f32[256,2,4,128]{0,3,2,1:T(8,128)}, f32[4,512,512]{2,1,0:T(8,128)}, bf16[4,512,2,128]{3,1,2,0:T(8,128)(2,1)}, s32[4,512]{1,0:T(4,12...) while((s32[]{:T(128)}, f32[256,2,4,128]{0,3,2,1:T(8,128)}, ...), condition=%wide.region_8.9_spmd.clone, body=%wide.region_7.8_spmd.clone.sunk | while | flops 1352925184 | bytes 31496380 | solution.py:154
  121.9 2.4 fusion.94
  124.3 1.9 fusion.97
  126.2 1.8 fusion.95
  128.1 1.8 fusion.98
  129.9 2.5 fusion.96
  133.5 1.6 copy.68
  136.3 2.4 fusion.94
  138.7 1.9 fusion.97
  140.6 1.8 fusion.95
  142.4 1.8 fusion.98
  144.3 2.9 fusion.96
  148.2 1.6 copy.68
  151.1 2.4 fusion.94
  153.5 1.9 fusion.97
  155.4 1.8 fusion.95
  157.2 1.8 fusion.98
  159.1 2.9 fusion.96
  163.0 1.6 copy.68
  165.9 2.4 fusion.94
  168.3 1.9 fusion.97
  170.2 1.8 fusion.95
  172.0 1.8 fusion.98
  173.9 2.9 fusion.96
  181.8 7.8 %fusion.34 = f32[256,4096]{1,0:T(8,128)} fusion(bf16[256,1024]{0,1:T(8,128)(2,1)S(1)} %bitcast.183, bf16[4096,1024]{1,0:T(8,128)(2,1)} %param.14), kind=kOutput, calls=%fused_computation.68 | convolution fusion | flops 2147483648 | bytes 13107200 | tf_op jit(solution)/shard_map/dot_general | solution.py:32
  189.6 42.4 %reduce-scatter.2.cloned.1.call-done = f32[256,512]{1,0:T(8,128)} async-done(((f32[2048,512]{1,0:T(8,128)}), f32[256,512]{1,0:T(8,128)}) %reduce-scatter.2.cloned.1.call-update) | async-done | bytes 524304 | tf_op jit(solution)/shard_map/reduce_scatter | solution.py:160
  233.0 3.1 convolution_add_fusion.1
  236.2 2.7 convolution_add_fusion
  238.8 147.4 %all-reduce.1 = bf16[256,4096]{1,0:T(8,128)(2,1)} all-reduce(f32[256,4096]{1,0:T(8,128)} %convolution_add_fusion), channel_id=1, replica_groups=mesh['head'=4,'ctx'=8] {'head'}, use_global_device_ids=true, to_apply=%region_10.11 | all-reduce | flops 1048576 | bytes 6291456 | tf_op jit(solution)/shard_map/psum | solution.py:170
  386.2 1.9 dynamic-slice_convert_fusion
  (88 shorter events, 27.6 us)
Async XLA Ops:
  6.5 1.6 copy-start
  6.5 51.1 %all-gather.5.cloned.1.call-start = ((), (), s32[]{:S(2)}) async-start(), calls=%async_computation.2 | async-start | bytes 2621440 | tf_op jit(solution)/shard_map/all_gather | solution.py:102
  7.3 5.5 %copy-start.5 = (s32[8]{0:T(128)S(1)}, s32[8]{0:T(128)}, u32[]{:S(2)}) copy-start(s32[8]{0:T(128)} %param.18) | copy-start | bytes 100
  7.3 5.7 %copy-start.6 = (s32[16]{0:T(128)S(1)}, s32[16]{0:T(128)}, u32[]{:S(2)}) copy-start(s32[16]{0:T(128)} %param.19) | copy-start | bytes 196
  7.3 79.1 %all-gather.3.cloned.1.call-start = ((), (), s32[]{:S(2)}) async-start(), calls=%async_computation.1 | async-start | bytes 2359296 | tf_op jit(solution)/shard_map/all_gather | solution.py:104
  8.1 2.7 copy-start.1
  8.1 2.9 copy-start.2
  12.7 219.3 %reduce-scatter.2.cloned.1.call-start = ((), (), s32[]{:S(2)}) async-start(), calls=%async_computation.3 | async-start | bytes 4718592 | tf_op jit(solution)/shard_map/reduce_scatter | solution.py:160
  91.0 9.0 %copy-start.4 = (bf16[256,2,4,128]{3,0,2,1:T(8,128)(2,1)S(1)}, bf16[256,2,4,128]{3,0,2,1:T(8,128)(2,1)}, u32[]{:S(2)}) copy-start(bf16[256,2,4,128]{3,0,2,1:T(8,128)(2,1)} %copy.43) | copy-start | bytes 1572868
  233.0 3.1 copy-start.3
Sparse Core Ops, SparseCore 0:
  8.9 48.6 all-gather.4
  59.5 26.9 all-gather.2
  180.6 51.3 reduce-scatter.1
where the time goes:
time: 396 us; the launch traced here: 395 us
  blocking collectives  147 us (37%)
  waiting for transfers between devices  97.6 us (25%)
  matrix products  90.1 us (23%)
  local copies, waits for them, and re-layouts  32.2 us (8%)
  other arithmetic  13.6 us (3%)
  between operations  13.3 us (3%)
    psum x1, blocking collectives, shards(): summed = lax.psum(partial_value, 'head')  147 us
    reduce_scatter x1, waiting for transfers between devices, shards(): lax.psum_scatter(lookup_pieces.reshape(length, -1), 'ctx', scatter_dimens...  42.4 us
    all_gather x1, waiting for transfers between devices, shards(): lax.all_gather(out_grad, 'head', axis=1, tiled=True)  36.2 us
    dot_general x4, matrix products, back_project(): lax.dot_general(grad, weight, (((1,), (1,)), ((), ())), preferred_element...  20.7 us
    all_gather x1, waiting for transfers between devices, shards(): lax.all_gather(jnp.concatenate([keys, values], axis=1), 'ctx', axis=0, ti...  18.2 us
    dot_general x8, matrix products, block_scores(): jnp.einsum('qagd,kad->agqk', query_part, key_part, preferred_element_type...  16.6 us
    dot_general x4, matrix products, key_side(): jnp.einsum('agqk,kad->qagd', score_grad, key_part, preferred_element_type...  11.2 us
    dynamic_update_slice x8, local copies, waits for them, and re-layouts, shards(): lax.scan(key_side, jnp.zeros((tokens, kv_heads, sharing_bundles, CHANNEL_...  10.5 us
  transfers between devices with their start and end apart: 3, of which 3 were waited for; matrix products, arithmetic and copies ran while one was open for 8% of the time, Pallas kernels for 0%

commit v1 on v0

v1 whole, which is shorter than its diff:
```python
import functools
import math

import jax
import jax.numpy as jnp
from jax import lax
from jax.experimental import pallas as pl
from jax.experimental.pallas import tpu as pltpu
from jax.sharding import PartitionSpec as P

ASKER_NUM = 32
SHARED_KV_NUM = 8
CHANNEL_DIM = 128

masked_score = -1e30
MIB = 1 << 20
VMEM = pltpu.VMEM


def mm(a, b):
    return lax.dot_general(a, b, (((1,), (0,)), ((), ())), preferred_element_type=jnp.float32)


def mm_nt(a, b):
    return lax.dot_general(a, b, (((1,), (1,)), ((), ())), preferred_element_type=jnp.float32)


def mm_tn(a, b):
    return lax.dot_general(a, b, (((0,), (0,)), ((), ())), preferred_element_type=jnp.float32)


def params(limit):
    return pltpu.CompilerParams(vmem_limit_bytes=limit * MIB)


def cost(flops, moved):
    return pl.CostEstimate(flops=flops, bytes_accessed=moved, transcendentals=0)


def kv_body(x_ref, wk_ref, wv_ref, out_ref, acc):
    width = wk_ref.shape[1]
    step = pl.program_id(0)

    @pl.when(step == 0)
    def _():
        acc[...] = jnp.zeros_like(acc)

    x = x_ref[...]
    acc[:, :width] += mm(x, wk_ref[...])
    acc[:, width:] += mm(x, wv_ref[...])

    @pl.when(step == pl.num_programs(0) - 1)
    def _():
        out_ref[...] = acc[...].astype(out_ref.dtype)


def project_kv(x, wk, wv):
    tokens, depth = x.shape
    width = wk.shape[1]
    part = min(depth, 1024)
    return pl.pallas_call(
        kv_body,
        grid=(depth // part,),
        in_specs=[
            pl.BlockSpec((tokens, part), lambda i: (0, i)),
            pl.BlockSpec((part, width), lambda i: (i, 0)),
            pl.BlockSpec((part, width), lambda i: (i, 0)),
        ],
        out_specs=pl.BlockSpec((tokens, 2 * width), lambda i: (0, 0)),
        out_shape=jax.ShapeDtypeStruct((tokens, 2 * width), jnp.bfloat16),
        scratch_shapes=[VMEM((tokens, 2 * width), jnp.float32)],
        compiler_params=params(24),
        cost_estimate=cost(4 * tokens * depth * width, 2 * depth * (tokens + 2 * width)),
        name="project_kv",
    )(x, wk, wv)


def project_body(x_ref, w_ref, out_ref):
    out_ref[...] = mm(x_ref[...], w_ref[...]).astype(out_ref.dtype)


def project(x, w):
    tokens, depth = x.shape
    width = w.shape[1]
    part = min(width, 256)
    return pl.pallas_call(
        project_body,
        grid=(width // part,),
        in_specs=[
            pl.BlockSpec((tokens, depth), lambda i: (0, 0)),
            pl.BlockSpec((depth, part), lambda i: (0, i)),
        ],
        out_specs=pl.BlockSpec((tokens, part), lambda i: (0, i)),
        out_shape=jax.ShapeDtypeStruct((tokens, width), jnp.bfloat16),
        compiler_params=params(24),
        cost_estimate=cost(2 * tokens * depth * width, 2 * depth * (tokens + width)),
        name="project",
    )(x, w)


def back_body(x_ref, w_ref, out_ref):
    out_ref[...] = mm_nt(x_ref[...], w_ref[...]).astype(out_ref.dtype)


def back_project(x, w):
    tokens, depth = x.shape
    width = w.shape[0]
    part = min(width, 256)
    return pl.pallas_call(
        back_body,
        grid=(width // part,),
        in_specs=[
            pl.BlockSpec((tokens, depth), lambda i: (0, 0)),
            pl.BlockSpec((part, depth), lambda i: (i, 0)),
        ],
        out_specs=pl.BlockSpec((tokens, part), lambda i: (0, i)),
        out_shape=jax.ShapeDtypeStruct((tokens, width), jnp.bfloat16),
        compiler_params=params(24),
        cost_estimate=cost(2 * tokens * depth * width, 2 * depth * (tokens + width)),
        name="back_project",
    )(x, w)


def input_body(count, dq_ref, *refs):
    terms = refs[:count]
    wq_ref, wk_ref, wv_ref, out_ref, grads = refs[count:]
    width = wk_ref.shape[1]

    @pl.when(pl.program_id(0) == 0)
    def _():
        total = terms[0][...].astype(jnp.float32)
        for term in terms[1:]:
            total = total + term[...].astype(jnp.float32)
        grads[...] = total.astype(grads.dtype)

    total = mm_nt(dq_ref[...], wq_ref[...])
    total = total + mm_nt(grads[:, :width], wk_ref[...])
    total = total + mm_nt(grads[:, width:], wv_ref[...])
    out_ref[...] = total.astype(out_ref.dtype)


def input_terms(dq, terms, wq, wk, wv):
    tokens, depth = dq.shape
    rows, width = wk.shape
    part = min(rows, 512)
    whole = lambda a: pl.BlockSpec(a.shape, lambda i: (0, 0))
    return pl.pallas_call(
        functools.partial(input_body, len(terms)),
        grid=(rows // part,),
        in_specs=[whole(dq)]
        + [whole(t) for t in terms]
        + [
            pl.BlockSpec((part, depth), lambda i: (i, 0)),
            pl.BlockSpec((part, width), lambda i: (i, 0)),
            pl.BlockSpec((part, width), lambda i: (i, 0)),
        ],
        out_specs=pl.BlockSpec((tokens, part), lambda i: (0, i)),
        out_shape=jax.ShapeDtypeStruct((tokens, rows), jnp.bfloat16),
        scratch_shapes=[VMEM((tokens, 2 * width), jnp.bfloat16)],
        compiler_params=params(24),
        cost_estimate=cost(
            2 * tokens * rows * (depth + 2 * width), 2 * rows * (tokens + depth + 2 * width)
        ),
        name="input_terms",
    )(dq, *terms, wq, wk, wv)


def find_places(order, places, me, spans):
    for i in range(spans):
        places[order[i]] = ((i // 2) ^ me) * 2 + (i % 2)


def own_span(order, lengths, docs, me, j, half):
    span = order[2 * me + j]
    position = span * half + lax.broadcasted_iota(jnp.int32, (1, half), 1)
    first, end = 0, 0
    start = jnp.zeros((1, half), jnp.int32)
    for k in range(docs):
        end = end + lengths[k]
        start = jnp.where(position >= end, end, start)
        first = jnp.where(span * half >= end, end, first)
    return span, position, start, first // half


def stack_heads(ref, rows, group, share, dim):
    base = group * share
    return jnp.concatenate(
        [ref[rows, (base + h) * dim : (base + h + 1) * dim] for h in range(share)], axis=0
    )


def load_blocks(refs, held):
    rows = refs[0].shape[0]
    for k, ref in enumerate(refs):
        held[k * rows : (k + 1) * rows, :] = ref[...]


def allowed_of(p, position, start, half, share):
    key = p * half + lax.broadcasted_iota(jnp.int32, (half, 1), 0)
    allowed = (key <= position) & (key >= start)
    return jnp.concatenate([allowed] * share, axis=1)


def stats_body(sizes, order, lengths, q_ref, *refs):
    peers, half, groups, share, dim, docs = sizes
    blocks = refs[:peers]
    level_ref, mixed_ref, held, places = refs[peers:]
    me = lax.axis_index("ctx")
    width = groups * dim
    factor = math.log2(math.e) / math.sqrt(dim)
    find_places(order, places, me, 2 * peers)
    load_blocks(blocks, held)
    columns = share * half
    for j in range(2):
        span, position, start, lowest = own_span(order, lengths, docs, me, j, half)
        rows = slice(j * half, (j + 1) * half)
        queries = [stack_heads(q_ref, rows, g, share, dim) for g in range(groups)]

        def visit(p, carry):
            place = pl.multiple_of(places[p] * half, half)
            allowed = allowed_of(p, position, start, half, share)
            fresh = []
            for g in range(groups):
                top, total, mixed = carry[g]
                keys = held[pl.ds(place, half), g * dim : (g + 1) * dim]
                values = held[pl.ds(place, half), width + g * dim : width + (g + 1) * dim]
                logits = mm_nt(keys, queries[g]) * factor
                logits = jnp.where(allowed, logits, masked_score)
                higher = jnp.maximum(top, jnp.max(logits, axis=0, keepdims=True))
                weights = jnp.where(allowed, jnp.exp2(logits - higher), 0.0)
                fade = jnp.exp2(top - higher)
                total = total * fade + jnp.sum(weights, axis=0, keepdims=True)
                mixed = mixed * fade + mm_tn(values, weights.astype(jnp.bfloat16))
                fresh.append((higher, total, mixed))
            return tuple(fresh)

        empty = (
            jnp.full((1, columns), masked_score, jnp.float32),
            jnp.zeros((1, columns), jnp.float32),
            jnp.zeros((dim, columns), jnp.float32),
        )
        done = lax.fori_loop(lowest, span + 1, visit, (empty,) * groups)
        for g in range(groups):
            top, total, mixed = done[g]
            level_ref[j * groups + g] = top + jnp.log2(total)
            mixed_ref[j * groups + g] = mixed / total


def stats(q, blocks, span_order, doc_lengths, sizes):
    peers, half, groups, share, dim, docs = sizes
    columns = share * half
    return pl.pallas_call(
        functools.partial(stats_body, sizes),
        in_specs=[pl.BlockSpec(memory_space=pltpu.SMEM)] * 2
        + [pl.BlockSpec(memory_space=VMEM)] * (1 + peers),
        out_specs=[pl.BlockSpec(memory_space=VMEM)] * 2,
        out_shape=[
            jax.ShapeDtypeStruct((2 * groups, 1, columns), jnp.float32),
            jax.ShapeDtypeStruct((2 * groups, dim, columns), jnp.float32),
        ],
        scratch_shapes=[
            VMEM((2 * peers * half, 2 * groups * dim), jnp.bfloat16),
            pltpu.SMEM((2 * peers,), jnp.int32),
        ],
        compiler_params=params(40),
        cost_estimate=cost(9 * peers * half * half * columns * groups * dim // dim, 6 * MIB),
        name="stats",
    )(span_order, doc_lengths, q, *blocks)


def grads_body(sizes, order, lengths, q_ref, g_ref, level_ref, mixed_ref, *refs):
    peers, half, groups, share, dim, docs = sizes
    blocks = refs[:peers]
    dq_ref, even_ref, odd_ref, held, sums, places = refs[peers:]
    me = lax.axis_index("ctx")
    width = groups * dim
    scale = 1.0 / math.sqrt(dim)
    factor = math.log2(math.e) * scale
    find_places(order, places, me, 2 * peers)
    load_blocks(blocks, held)
    sums[...] = jnp.zeros_like(sums)
    columns = share * half
    for j in range(2):
        span, position, start, lowest = own_span(order, lengths, docs, me, j, half)
        rows = slice(j * half, (j + 1) * half)
        queries = [stack_heads(q_ref, rows, g, share, dim) for g in range(groups)]
        outs = [stack_heads(g_ref, rows, g, share, dim) for g in range(groups)]
        levels = [level_ref[j * groups + g] for g in range(groups)]
        deltas = []
        for g in range(groups):
            turned = jnp.concatenate(
                [
                    outs[g][h * half : (h + 1) * half].astype(jnp.float32).T
                    for h in range(share)
                ],
                axis=1,
            )
            deltas.append(jnp.sum(turned * mixed_ref[j * groups + g], axis=0, keepdims=True))

        def visit(p, carry):
            place = pl.multiple_of(places[p] * half, half)
            allowed = allowed_of(p, position, start, half, share)
            fresh = []
            for g in range(groups):
                keys = held[pl.ds(place, half), g * dim : (g + 1) * dim]
                values = held[pl.ds(place, half), width + g * dim : width + (g + 1) * dim]
                logits = mm_nt(keys, queries[g]) * factor
                chance = jnp.where(allowed, jnp.exp2(logits - levels[g]), 0.0)
                slopes = mm_nt(values, outs[g])
                score = (chance * (slopes - deltas[g])).astype(jnp.bfloat16)
                sums[pl.ds(place, half), g * dim : (g + 1) * dim] += mm(score, queries[g])
                sums[pl.ds(place, half), width + g * dim : width + (g + 1) * dim] += mm(
                    chance.astype(jnp.bfloat16), outs[g]
                )
                fresh.append(carry[g] + mm_tn(keys, score))
            return tuple(fresh)

        empty = jnp.zeros((dim, columns), jnp.float32)
        done = lax.fori_loop(lowest, span + 1, visit, (empty,) * groups)
        for g in range(groups):
            for h in range(share):
                head = g * share + h
                dq_ref[rows, head * dim : (head + 1) * dim] = (
                    (done[g][:, h * half : (h + 1) * half].T * scale).astype(dq_ref.dtype)
                )
    tokens = 2 * half
    for k in range(peers):
        out, at = (even_ref, odd_ref)[k % 2], k // 2
        part = sums[k * tokens : (k + 1) * tokens, :]
        out[at, :, :width] = (part[:, :width] * scale).astype(out.dtype)
        out[at, :, width:] = part[:, width:].astype(out.dtype)


def grads(q, g, level, mixed, blocks, span_order, doc_lengths, sizes):
    peers, half, groups, share, dim, docs = sizes
    tokens, width = 2 * half, groups * dim
    columns = share * half
    terms = jax.ShapeDtypeStruct((peers // 2, tokens, 2 * width), jnp.bfloat16)
    return pl.pallas_call(
        functools.partial(grads_body, sizes),
        in_specs=[pl.BlockSpec(memory_space=pltpu.SMEM)] * 2
        + [pl.BlockSpec(memory_space=VMEM)] * (4 + peers),
        out_specs=[pl.BlockSpec(memory_space=VMEM)] * 3,
        out_shape=[jax.ShapeDtypeStruct(q.shape, jnp.bfloat16), terms, terms],
        scratch_shapes=[
            VMEM((peers * tokens, 2 * width), jnp.bfloat16),
            VMEM((peers * tokens, 2 * width), jnp.float32),
            pltpu.SMEM((2 * peers,), jnp.int32),
        ],
        compiler_params=params(48),
        cost_estimate=cost(18 * peers * half * half * columns * groups, 12 * MIB),
        name="grads",
    )(span_order, doc_lengths, q, g, level, mixed, *blocks)


def swap(x, k, size):
    return lax.ppermute(x, "ctx", [(i, i ^ k) for i in range(size)])


def gather_ctx(x):
    size = lax.axis_size("ctx")
    even = [x] + [swap(x, k, size) for k in range(2, size, 2)]
    odd = [swap(block, 1, size) for block in even]
    return [block for pair in zip(even, odd) for block in pair]


def pair_body(even_ref, odd_ref, *outs):
    for k, out in enumerate(outs):
        out[...] = (
            even_ref[k].astype(jnp.float32) + odd_ref[k].astype(jnp.float32)
        ).astype(out.dtype)


def scatter_ctx(even, odd):
    size = lax.axis_size("ctx")
    count, rows, width = even.shape
    got = swap(odd, 1, size)
    pairs = pl.pallas_call(
        pair_body,
        in_specs=[pl.BlockSpec(memory_space=VMEM)] * 2,
        out_specs=[pl.BlockSpec(memory_space=VMEM)] * count,
        out_shape=[jax.ShapeDtypeStruct((rows, width), jnp.bfloat16)] * count,
        compiler_params=params(24),
        cost_estimate=cost(even.size, 6 * even.size),
        name="pair_sums",
    )(even, got)
    return [pairs[0]] + [swap(pairs[k], 2 * k, size) for k in range(1, count)]


def shards(inputs, out_grad, w_query, w_key, value_projection, w_out, doc_lengths, span_order):
    tokens = inputs.shape[0]
    share = ASKER_NUM // SHARED_KV_NUM
    sizes = (
        lax.axis_size("ctx"),
        tokens // 2,
        w_key.shape[1] // CHANNEL_DIM,
        share,
        CHANNEL_DIM,
        doc_lengths.shape[0],
    )
    gathered = lax.all_gather(out_grad, "head", axis=1, tiled=True)
    own = project_kv(inputs, w_key, value_projection)
    blocks = gather_ctx(own)
    query = project(inputs, w_query)
    level, mixed = stats(query, blocks, span_order, doc_lengths, sizes)
    context_grad = back_project(gathered, w_out)
    query_grad, even, odd = grads(
        query, context_grad, level, mixed, blocks, span_order, doc_lengths, sizes
    )
    terms = scatter_ctx(even, odd)
    partial_value = input_terms(query_grad, terms, w_query, w_key, value_projection)
    return lax.psum_scatter(partial_value, "head", scatter_dimension=1, tiled=True)


def solution(mesh):
    in_specs = (
        P("ctx", None),
        P("ctx", "head"),
        P(None, "head"),
        P(None, "head"),
        P(None, "head"),
        P("head", None),
        P(),
        P(),
    )
    out_specs = P("ctx", "head")
    return jax.shard_map(shards, mesh=mesh, in_specs=in_specs, out_specs=out_specs, check_vma=False)
```

time: 396 us -> 151 us (0.38)
  blocking collectives: 147 us -> 0 us
  matrix products: 90.1 us -> 0 us
  Pallas kernels: 0 us -> 31.7 us
  waiting for transfers between devices: 97.6 us -> 76.2 us
  other arithmetic: 13.6 us -> 0.01 us
  local copies, waits for them, and re-layouts: 32.2 us -> 19.1 us
  starting transfers between devices: 0.08 us -> 11.1 us
    psum x1 -> x0, blocking collectives: 147 us -> none  [shards(): summed = lax.psum(partial_value, 'head')]
    dot_general x35 -> x0, matrix products: 90.1 us -> none  [the longest x4 20.7 us: back_project(): lax.dot_general(grad, weight, (((1,), (1,)), ((), ())), preferred_element...]
    all_gather x2 -> x1, waiting for transfers between devices: 54.4 us -> 7.34 us  [shards(): gathered = lax.all_gather(out_grad, 'head', axis=1, tiled=True)]
    pallas_call x0 -> x7, Pallas kernels: none -> 31.7 us  [the longest x1 9.64 us: grads(): pl.pallas_call(functools.partial(grads_body, sizes), in_specs=[pl.BlockSp...]
    ppermute x0 -> x11, waiting for transfers between devices: none -> 26 us  [swap(): return lax.ppermute(x, 'ctx', [(i, i ^ k) for i in range(size)])]
    ppermute x0 -> x11, starting transfers between devices: none -> 11.1 us  [swap(): return lax.ppermute(x, 'ctx', [(i, i ^ k) for i in range(size)])]
    dynamic_update_slice x8 -> x0, local copies, waits for them, and re-layouts: 10.5 us -> none  [shards(): lax.scan(key_side, jnp.zeros((tokens, kv_heads, sharing_bundles, CHANNEL_...]
    unnamed x21 -> x60, local copies, waits for them, and re-layouts: 9.57 us -> 19.1 us
  transfers between devices with their start and end apart: 3 -> 13, of which waited for: 3 -> 9; matrix products, arithmetic and copies ran while one was open for 8% -> 0% of each run, Pallas kernels for 0% -> 9%
where the time goes in v1:
time: 151 us; the launch traced here: 152 us
  waiting for transfers between devices  76.2 us (50%)
  Pallas kernels  31.7 us (21%)
  local copies, waits for them, and re-layouts  19.1 us (13%)
  between operations  13.7 us (9%)
  starting transfers between devices  11.1 us (7%)
    reduce_scatter x1, waiting for transfers between devices, shards(): lax.psum_scatter(partial_value, 'head', scatter_dimension=1, tiled=True)  42.1 us
    ppermute x11, waiting for transfers between devices, swap(): return lax.ppermute(x, 'ctx', [(i, i ^ k) for i in range(size)])  26 us
    unnamed x60, local copies, waits for them, and re-layouts  19.1 us
    ppermute x11, starting transfers between devices, swap(): return lax.ppermute(x, 'ctx', [(i, i ^ k) for i in range(size)])  11.1 us
    pallas_call x1, Pallas kernels, grads(): pl.pallas_call(functools.partial(grads_body, sizes), in_specs=[pl.BlockSp...  9.64 us
    pallas_call x1, Pallas kernels, stats(): pl.pallas_call(functools.partial(stats_body, sizes), in_specs=[pl.BlockSp...  7.6 us
    all_gather x1, waiting for transfers between devices, shards(): gathered = lax.all_gather(out_grad, 'head', axis=1, tiled=True)  7.34 us
    pallas_call x1, Pallas kernels, input_terms(): pl.pallas_call(functools.partial(input_body, len(terms)), grid=(rows // p...  5.14 us
  transfers between devices with their start and end apart: 13, of which 9 were waited for; matrix products, arithmetic and copies ran while one was open for 0% of the time, Pallas kernels for 9%

profile of v1, /device:TPU:0, one launch (start us, length us, event | category | flops | bytes accessed | tf_op | source)
XLA Modules:
  0.0 151.9 jit_solution(4832015478229478961)
XLA Ops:
  6.5 0.7 all-gather.2.cloned.1.call-update
  7.3 0.0 reduce-scatter.2.cloned.1.call-start
  7.3 1.6 %copy-done.2 = bf16[256,4096]{1,0:T(8,128)(2,1)S(1)} copy-done((bf16[256,4096]{1,0:T(8,128)(2,1)S(1)}, bf16[256,4096]{1,0:T(8,128)(2,1)}, u32[]{:S(2)}) %copy-start.2) | copy-done | bytes 2097176
  8.9 1.6 %copy-done.3 = bf16[4096,256]{1,0:T(8,128)(2,1)S(1)} copy-done((bf16[4096,256]{1,0:T(8,128)(2,1)S(1)}, bf16[4096,256]{1,0:T(8,128)(2,1)}, u32[]{:S(2)}) %copy-start.3) | copy-done | bytes 2097176
  10.5 1.6 %copy-done.5 = bf16[4096,256]{1,0:T(8,128)(2,1)S(1)} copy-done((bf16[4096,256]{1,0:T(8,128)(2,1)S(1)}, bf16[4096,256]{1,0:T(8,128)(2,1)}, u32[]{:S(2)}) %copy-start.5) | copy-done | bytes 2097176
  12.1 2.0 %project_kv.1.refs_0_ = bf16[256,512]{1,0:T(8,128)(2,1)S(1)} custom-call(bf16[256,4096]{1,0:T(8,128)(2,1)S(1)} %copy-done.2, bf16[4096,256]{1,0:T(8,128)(2,1)S(1)} %copy-done.3, bf16[4096,256]{1,0:T(8,128)(2,1)S(1)} %copy-done.5), custom_call_target="tpu_custom_call" | custom-call | flops 1073741824 | bytes 6291456 | tf_op jit(solution)/shard_map/project_kv/pallas_call | solution.py:61
  14.1 4.0 %collective-permute-start.5 = (bf16[256,512]{1,0:T(8,128)(2,1)S(1)}, bf16[256,512]{1,0:T(8,128)(2,1)S(1)}, u32[]{:S(2)}, u32[]{:S(2)}) collective-permute-start(bf16[256,512]{1,0:T(8,128)(2,1)S(1)} %project_kv.1.refs_0_), channel_id=1, source_target_pairs={{0,6},{1,7},{2,4},{3,5},{4,2},{5,3},{6,0},{7,1},{8,14},{9,15},{10,... | collective-permute-start | bytes 786440 | tf_op jit(solution)/shard_map/ppermute | solution.py:357
  18.1 0.5 collective-permute-start.3
  18.6 0.1 collective-permute-start.1
  18.7 0.0 collective-permute-start
  18.7 6.5 %collective-permute-done.5.refs_6_ = bf16[256,512]{1,0:T(8,128)(2,1)S(1)} collective-permute-done((bf16[256,512]{1,0:T(8,128)(2,1)S(1)}, bf16[256,512]{1,0:T(8,128)(2,1)S(1)}, u32[]{:S(2)}, u32[]{:S(2)}) %collective-permute-start.5) | collective-permute-done | bytes 262176 | tf_op jit(solution)/shard_map/ppermute | solution.py:357
  25.3 0.0 collective-permute-start.6
  25.3 4.7 %collective-permute-done.3.refs_4_ = bf16[256,512]{1,0:T(8,128)(2,1)S(1)} collective-permute-done((bf16[256,512]{1,0:T(8,128)(2,1)S(1)}, bf16[256,512]{1,0:T(8,128)(2,1)S(1)}, u32[]{:S(2)}, u32[]{:S(2)}) %collective-permute-start.3) | collective-permute-done | bytes 262176 | tf_op jit(solution)/shard_map/ppermute | solution.py:357
  30.0 0.1 collective-permute-start.4
  30.1 0.2 collective-permute-done.1.refs_2_
  30.3 0.2 collective-permute-start.2
  30.5 3.4 %copy-done = bf16[4096,1024]{1,0:T(8,128)(2,1)S(1)} copy-done((bf16[4096,1024]{1,0:T(8,128)(2,1)S(1)}, bf16[4096,1024]{1,0:T(8,128)(2,1)}, u32[]{:S(2)}) %copy-start) | copy-done | bytes 8388632
  33.9 4.0 %project.1.q_ref = bf16[256,1024]{1,0:T(8,128)(2,1)S(1)} custom-call(bf16[256,4096]{1,0:T(8,128)(2,1)S(1)} %copy-done.2, bf16[4096,1024]{1,0:T(8,128)(2,1)S(1)} %copy-done), custom_call_target="tpu_custom_call" | custom-call | flops 2147483648 | bytes 10485760 | tf_op jit(solution)/shard_map/project/pallas_call | solution.py:86
  38.1 7.6 %stats.1 = (f32[4,1,512]{2,1,0:T(1,128)S(1)}, f32[4,128,512]{2,1,0:T(8,128)S(1)}) custom-call(s32[16]{0:T(128)S(1)} %copy-done.25, s32[8]{0:T(128)S(1)} %copy-done.26, bf16[256,1024]{1,0:T(8,128)(2,1)S(1)} %project.1.q_ref, bf16[256,512]{1,0:T(8,128)(2,1)S(1)} %project_kv.1.refs_0_, bf16[256,512]{1,0:T(8,128)(2,1)S(1)} %collective-permute-done.refs_1_, ...), custom_call_target="tpu_custom_call" | custom-call | flops 1207959552 | bytes 6291456 | tf_op jit(solution)/shard_map/stats/pallas_call | solution.py:252
  45.7 0.0 copy-start.9
  45.7 0.8 copy-done.9
  46.5 0.7 copy-done.17
  47.2 0.7 copy-done.19
  47.9 0.7 copy-done.21
  48.6 0.7 copy-done.23
  49.3 1.0 copy-done.27
  50.3 7.3 %all-gather.2.cloned.1.call-done.x_ref = bf16[256,4096]{1,0:T(8,128)(2,1)} async-done(((bf16[256,1024]{1,0:T(8,128)(2,1)}), bf16[256,4096]{1,0:T(8,128)(2,1)}) %all-gather.2.cloned.1.call-update) | async-done | bytes 2097168 | tf_op jit(solution)/shard_map/all_gather | solution.py:401
  57.6 3.4 %copy-done.1 = bf16[1024,4096]{1,0:T(8,128)(2,1)S(1)} copy-done((bf16[1024,4096]{1,0:T(8,128)(2,1)S(1)}, bf16[1024,4096]{1,0:T(8,128)(2,1)}, u32[]{:S(2)}) %copy-start.1) | copy-done | bytes 8388632
  61.0 1.6 %copy-done.8 = bf16[256,4096]{1,0:T(8,128)(2,1)S(1)} copy-done((bf16[256,4096]{1,0:T(8,128)(2,1)S(1)}, bf16[256,4096]{1,0:T(8,128)(2,1)}, u32[]{:S(2)}) %copy-start.8) | copy-done | bytes 2097176
  62.6 0.0 slice-start
  62.6 3.1 %back_project.1.g_ref = bf16[256,1024]{1,0:T(8,128)(2,1)S(1)} custom-call(bf16[256,4096]{1,0:T(8,128)(2,1)S(1)} %copy-done.8, bf16[1024,4096]{1,0:T(8,128)(2,1)S(1)} %copy-done.1), custom_call_target="tpu_custom_call" | custom-call | flops 2147483648 | bytes 10485760 | tf_op jit(solution)/shard_map/back_project/pallas_call | solution.py:109
  65.8 0.0 slice-start.1
  65.8 0.0 copy-start.6
  65.8 9.6 %grads.1 = (bf16[256,1024]{1,0:T(8,128)(2,1)S(1)}, bf16[4,256,512]{2,1,0:T(8,128)(2,1)S(1)}, bf16[4,256,512]{2,1,0:T(8,128)(2,1)S(1)}) custom-call(s32[16]{0:T(128)S(1)} %copy-done.25, s32[8]{0:T(128)S(1)} %copy-done.26, bf16[256,1024]{1,0:T(8,128)(2,1)S(1)} %copy-done.10, bf16[256,1024]{1,0:T(8,128)(2,1)S(1)} %back_project.1.g_ref, ...), custom_call_target="tpu_custom_call" | custom-call | flops 2415919104 | bytes 12582912 | tf_op jit(solution)/shard_map/grads/pallas_call | solution.py:339
  75.5 0.0 copy-start.4
  75.5 0.1 collective-permute-start.7
  75.6 2.6 %collective-permute-done.7.odd_ref = bf16[4,256,512]{2,1,0:T(8,128)(2,1)S(1)} collective-permute-done((bf16[4,256,512]{2,1,0:T(8,128)(2,1)S(1)}, bf16[4,256,512]{2,1,0:T(8,128)(2,1)S(1)}, u32[]{:S(2)}, u32[]{:S(2)}) %collective-permute-start.7) | collective-permute-done | bytes 1048608 | tf_op jit(solution)/shard_map/ppermute | solution.py:357
  78.2 0.2 pair_sums.1
  78.5 1.5 %collective-permute-start.8 = (bf16[256,512]{1,0:T(8,128)(2,1)S(1)}, bf16[256,512]{1,0:T(8,128)(2,1)S(1)}, u32[]{:S(2)}, u32[]{:S(2)}) collective-permute-start(bf16[256,512]{1,0:T(8,128)(2,1)S(1)} %get-tuple-element.20), channel_id=1, source_target_pairs={{0,2},{1,3},{2,0},{3,1},{4,6},{5,7},{6,4},{7,5},{8,10},{9,11},{10,... | collective-permute-start | bytes 786440 | tf_op jit(solution)/shard_map/ppermute | solution.py:357
  80.0 3.1 %collective-permute-start.9 = (bf16[256,512]{1,0:T(8,128)(2,1)S(1)}, bf16[256,512]{1,0:T(8,128)(2,1)S(1)}, u32[]{:S(2)}, u32[]{:S(2)}) collective-permute-start(bf16[256,512]{1,0:T(8,128)(2,1)S(1)} %get-tuple-element.21), channel_id=1, source_target_pairs={{0,4},{1,5},{2,6},{3,7},{4,0},{5,1},{6,2},{7,3},{8,12},{9,13},{10,... | collective-permute-start | bytes 786440 | tf_op jit(solution)/shard_map/ppermute | solution.py:357
  83.1 1.4 collective-permute-start.10
  84.5 3.2 %collective-permute-done.8.refs_1_ = bf16[256,512]{1,0:T(8,128)(2,1)S(1)} collective-permute-done((bf16[256,512]{1,0:T(8,128)(2,1)S(1)}, bf16[256,512]{1,0:T(8,128)(2,1)S(1)}, u32[]{:S(2)}, u32[]{:S(2)}) %collective-permute-start.8) | collective-permute-done | bytes 262176 | tf_op jit(solution)/shard_map/ppermute | solution.py:357
  87.7 6.9 %collective-permute-done.9.refs_2_ = bf16[256,512]{1,0:T(8,128)(2,1)S(1)} collective-permute-done((bf16[256,512]{1,0:T(8,128)(2,1)S(1)}, bf16[256,512]{1,0:T(8,128)(2,1)S(1)}, u32[]{:S(2)}, u32[]{:S(2)}) %collective-permute-start.9) | collective-permute-done | bytes 262176 | tf_op jit(solution)/shard_map/ppermute | solution.py:357
  94.6 1.8 %collective-permute-done.10.refs_3_ = bf16[256,512]{1,0:T(8,128)(2,1)S(1)} collective-permute-done((bf16[256,512]{1,0:T(8,128)(2,1)S(1)}, bf16[256,512]{1,0:T(8,128)(2,1)S(1)}, u32[]{:S(2)}, u32[]{:S(2)}) %collective-permute-start.10) | collective-permute-done | bytes 262176 | tf_op jit(solution)/shard_map/ppermute | solution.py:357
  96.5 5.1 %input_terms.1 = bf16[256,4096]{1,0:T(8,128)(2,1)S(1)} custom-call(bf16[256,1024]{1,0:T(8,128)(2,1)S(1)} %get-tuple-element.16.dq_ref, bf16[256,512]{1,0:T(8,128)(2,1)S(1)} %get-tuple-element.19.refs_0_, bf16[256,512]{1,0:T(8,128)(2,1)S(1)} %collective-permute-done.8.refs_1_, bf16[256,512]{1,0:T(8,128)(2,1)S(1)} %collective-permute-done.9.refs_2_, ...), custom_call_target="tpu_custom_call" | custom-call | flops 3221225472 | bytes 14680064 | tf_op jit(solution)/shard_map/input_terms/pallas_call | solution.py:147
  101.6 1.3 copy-done.7
  103.0 0.0 reduce-scatter.2.cloned.1.call-update
  103.0 42.1 %reduce-scatter.2.cloned.1.call-done = bf16[256,1024]{1,0:T(8,128)(2,1)} async-done(((bf16[256,4096]{1,0:T(8,128)(2,1)}), bf16[256,1024]{1,0:T(8,128)(2,1)}) %reduce-scatter.2.cloned.1.call-update) | async-done | bytes 524304 | tf_op jit(solution)/shard_map/reduce_scatter | solution.py:412
  (48 shorter events, 0.1 us)
Async XLA Ops:
  6.5 51.1 %all-gather.2.cloned.1.call-start = ((), (), s32[]{:S(2)}) async-start(), calls=%async_computation.1 | async-start | bytes 2621440 | tf_op jit(solution)/shard_map/all_gather | solution.py:401
  7.3 137.9 %reduce-scatter.2.cloned.1.call-start = ((), (), s32[]{:S(2)}) async-start(), calls=%async_computation.2 | async-start | bytes 2621440 | tf_op jit(solution)/shard_map/reduce_scatter | solution.py:412
  7.3 1.6 %copy-start.2 = (bf16[256,4096]{1,0:T(8,128)(2,1)S(1)}, bf16[256,4096]{1,0:T(8,128)(2,1)}, u32[]{:S(2)}) copy-start(bf16[256,4096]{1,0:T(8,128)(2,1)} %x_ref.3) | copy-start | bytes 6291460
  8.9 1.6 %copy-start.3 = (bf16[4096,256]{1,0:T(8,128)(2,1)S(1)}, bf16[4096,256]{1,0:T(8,128)(2,1)}, u32[]{:S(2)}) copy-start(bf16[4096,256]{1,0:T(8,128)(2,1)} %refs_5_.1) | copy-start | bytes 6291460
  10.5 1.6 %copy-start.5 = (bf16[4096,256]{1,0:T(8,128)(2,1)S(1)}, bf16[4096,256]{1,0:T(8,128)(2,1)}, u32[]{:S(2)}) copy-start(bf16[4096,256]{1,0:T(8,128)(2,1)} %refs_6_.1) | copy-start | bytes 6291460
  12.1 26.0 %copy-start.25 = (s32[16]{0:T(128)S(1)}, s32[16]{0:T(128)}, u32[]{:S(2)}) copy-start(s32[16]{0:T(128)} %order.3) | copy-start | bytes 196
  12.1 26.0 %copy-start.26 = (s32[8]{0:T(128)S(1)}, s32[8]{0:T(128)}, u32[]{:S(2)}) copy-start(s32[8]{0:T(128)} %lengths.3) | copy-start | bytes 100
  14.1 11.1 %collective-permute-start.5 = (bf16[256,512]{1,0:T(8,128)(2,1)S(1)}, bf16[256,512]{1,0:T(8,128)(2,1)S(1)}, u32[]{:S(2)}, u32[]{:S(2)}) collective-permute-start(bf16[256,512]{1,0:T(8,128)(2,1)S(1)} %project_kv.1.refs_0_), channel_id=1, source_target_pairs={{0,6},{1,7},{2,4},{3,5},{4,2},{5,3},{6,0},{7,1},{8,14},{9,15},{10,... | collective-permute-start | bytes 786440 | tf_op jit(solution)/shard_map/ppermute | solution.py:357
  18.1 11.9 %collective-permute-start.3 = (bf16[256,512]{1,0:T(8,128)(2,1)S(1)}, bf16[256,512]{1,0:T(8,128)(2,1)S(1)}, u32[]{:S(2)}, u32[]{:S(2)}) collective-permute-start(bf16[256,512]{1,0:T(8,128)(2,1)S(1)} %project_kv.1.refs_0_), channel_id=1, source_target_pairs={{0,4},{1,5},{2,6},{3,7},{4,0},{5,1},{6,2},{7,3},{8,12},{9,13},{10,... | collective-permute-start | bytes 786440 | tf_op jit(solution)/shard_map/ppermute | solution.py:357
  18.6 11.7 %collective-permute-start.1 = (bf16[256,512]{1,0:T(8,128)(2,1)S(1)}, bf16[256,512]{1,0:T(8,128)(2,1)S(1)}, u32[]{:S(2)}, u32[]{:S(2)}) collective-permute-start(bf16[256,512]{1,0:T(8,128)(2,1)S(1)} %project_kv.1.refs_0_), channel_id=1, source_target_pairs={{0,2},{1,3},{2,0},{3,1},{4,6},{5,7},{6,4},{7,5},{8,10},{9,11},{10,... | collective-permute-start | bytes 786440 | tf_op jit(solution)/shard_map/ppermute | solution.py:357
  18.7 19.2 %collective-permute-start = (bf16[256,512]{1,0:T(8,128)(2,1)S(1)}, bf16[256,512]{1,0:T(8,128)(2,1)S(1)}, u32[]{:S(2)}, u32[]{:S(2)}) collective-permute-start(bf16[256,512]{1,0:T(8,128)(2,1)S(1)} %project_kv.1.refs_0_), channel_id=1, source_target_pairs={{0,1},{1,0},{2,3},{3,2},{4,5},{5,4},{6,7},{7,6},{8,9},{9,8},{10,11... | collective-permute-start | bytes 786440 | tf_op jit(solution)/shard_map/ppermute | solution.py:357
  25.2 12.8 %copy-start.11 = (bf16[256,512]{1,0:T(8,128)(2,1)}, bf16[256,512]{1,0:T(8,128)(2,1)S(1)}, u32[]{:S(2)}) copy-start(bf16[256,512]{1,0:T(8,128)(2,1)S(1)} %collective-permute-done.5.refs_6_) | copy-start | bytes 786436
  25.3 12.7 %collective-permute-start.6 = (bf16[256,512]{1,0:T(8,128)(2,1)S(1)}, bf16[256,512]{1,0:T(8,128)(2,1)S(1)}, u32[]{:S(2)}, u32[]{:S(2)}) collective-permute-start(bf16[256,512]{1,0:T(8,128)(2,1)S(1)} %collective-permute-done.5.refs_6_), channel_id=1, source_target_pairs={{0,1},{1,0},{2,3},{3,2},{4,5},{5,4},{6,7},{7,6},{8,9},{9,8},{10,11... | collective-permute-start | bytes 786440 | tf_op jit(solution)/shard_map/ppermute | solution.py:357
  30.0 8.0 %copy-start.13 = (bf16[256,512]{1,0:T(8,128)(2,1)}, bf16[256,512]{1,0:T(8,128)(2,1)S(1)}, u32[]{:S(2)}) copy-start(bf16[256,512]{1,0:T(8,128)(2,1)S(1)} %collective-permute-done.3.refs_4_) | copy-start | bytes 786436
  30.0 8.0 %collective-permute-start.4 = (bf16[256,512]{1,0:T(8,128)(2,1)S(1)}, bf16[256,512]{1,0:T(8,128)(2,1)S(1)}, u32[]{:S(2)}, u32[]{:S(2)}) collective-permute-start(bf16[256,512]{1,0:T(8,128)(2,1)S(1)} %collective-permute-done.3.refs_4_), channel_id=1, source_target_pairs={{0,1},{1,0},{2,3},{3,2},{4,5},{5,4},{6,7},{7,6},{8,9},{9,8},{10,11... | collective-permute-start | bytes 786440 | tf_op jit(solution)/shard_map/ppermute | solution.py:357
  30.3 7.7 %copy-start.15 = (bf16[256,512]{1,0:T(8,128)(2,1)}, bf16[256,512]{1,0:T(8,128)(2,1)S(1)}, u32[]{:S(2)}) copy-start(bf16[256,512]{1,0:T(8,128)(2,1)S(1)} %collective-permute-done.1.refs_2_) | copy-start | bytes 786436
  30.3 7.7 %collective-permute-start.2 = (bf16[256,512]{1,0:T(8,128)(2,1)S(1)}, bf16[256,512]{1,0:T(8,128)(2,1)S(1)}, u32[]{:S(2)}, u32[]{:S(2)}) collective-permute-start(bf16[256,512]{1,0:T(8,128)(2,1)S(1)} %collective-permute-done.1.refs_2_), channel_id=1, source_target_pairs={{0,1},{1,0},{2,3},{3,2},{4,5},{5,4},{6,7},{7,6},{8,9},{9,8},{10,11... | collective-permute-start | bytes 786440 | tf_op jit(solution)/shard_map/ppermute | solution.py:357
  30.5 3.4 %copy-start = (bf16[4096,1024]{1,0:T(8,128)(2,1)S(1)}, bf16[4096,1024]{1,0:T(8,128)(2,1)}, u32[]{:S(2)}) copy-start(bf16[4096,1024]{1,0:T(8,128)(2,1)} %refs_4_.1) | copy-start | bytes 25165828
  45.7 0.8 copy-start.9
  46.5 0.7 copy-start.17
  47.2 0.7 copy-start.19
  47.9 0.7 copy-start.21
  48.6 0.7 copy-start.23
  49.3 1.0 copy-start.27
  57.6 3.4 %copy-start.1 = (bf16[1024,4096]{1,0:T(8,128)(2,1)S(1)}, bf16[1024,4096]{1,0:T(8,128)(2,1)}, u32[]{:S(2)}) copy-start(bf16[1024,4096]{1,0:T(8,128)(2,1)} %w_ref.3) | copy-start | bytes 25165828
  61.0 1.6 %copy-start.8 = (bf16[256,4096]{1,0:T(8,128)(2,1)S(1)}, bf16[256,4096]{1,0:T(8,128)(2,1)}, u32[]{:S(2)}) copy-start(bf16[256,4096]{1,0:T(8,128)(2,1)} %all-gather.2.cloned.1.call-done.x_ref) | copy-start | bytes 6291460
  62.6 3.1 %copy-start.10 = (bf16[256,1024]{1,0:T(8,128)(2,1)S(1)}, bf16[256,1024]{1,0:T(8,128)(2,1)}, u32[]{:S(2)}) copy-start(bf16[256,1024]{1,0:T(8,128)(2,1)} %copy-done.9) | copy-start | bytes 1572868
  62.6 3.2 %copy-start.12 = (bf16[256,512]{1,0:T(8,128)(2,1)S(1)}, bf16[256,512]{1,0:T(8,128)(2,1)}, u32[]{:S(2)}) copy-start(bf16[256,512]{1,0:T(8,128)(2,1)} %copy-done.11) | copy-start | bytes 786436
  62.6 3.2 %copy-start.14 = (bf16[256,512]{1,0:T(8,128)(2,1)S(1)}, bf16[256,512]{1,0:T(8,128)(2,1)}, u32[]{:S(2)}) copy-start(bf16[256,512]{1,0:T(8,128)(2,1)} %copy-done.13) | copy-start | bytes 786436
  62.6 3.2 %copy-start.16 = (bf16[256,512]{1,0:T(8,128)(2,1)S(1)}, bf16[256,512]{1,0:T(8,128)(2,1)}, u32[]{:S(2)}) copy-start(bf16[256,512]{1,0:T(8,128)(2,1)} %copy-done.15) | copy-start | bytes 786436
  62.6 3.2 %copy-start.18 = (bf16[256,512]{1,0:T(8,128)(2,1)S(1)}, bf16[256,512]{1,0:T(8,128)(2,1)}, u32[]{:S(2)}) copy-start(bf16[256,512]{1,0:T(8,128)(2,1)} %copy-done.17) | copy-start | bytes 786436
  62.6 3.2 %copy-start.20 = (bf16[256,512]{1,0:T(8,128)(2,1)S(1)}, bf16[256,512]{1,0:T(8,128)(2,1)}, u32[]{:S(2)}) copy-start(bf16[256,512]{1,0:T(8,128)(2,1)} %copy-done.19) | copy-start | bytes 786436
  62.6 3.2 %copy-start.22 = (bf16[256,512]{1,0:T(8,128)(2,1)S(1)}, bf16[256,512]{1,0:T(8,128)(2,1)}, u32[]{:S(2)}) copy-start(bf16[256,512]{1,0:T(8,128)(2,1)} %copy-done.21) | copy-start | bytes 786436
  62.6 3.2 %copy-start.24 = (bf16[256,512]{1,0:T(8,128)(2,1)S(1)}, bf16[256,512]{1,0:T(8,128)(2,1)}, u32[]{:S(2)}) copy-start(bf16[256,512]{1,0:T(8,128)(2,1)} %copy-done.23) | copy-start | bytes 786436
  62.6 33.8 %slice-start = ((s8[8388608]{0:T(1024)(128)(4,1)}), s8[4194304]{0:T(1024)(128)(4,1)S(1)}, s32[]{:S(2)}) async-start(s8[8388608]{0:T(1024)(128)(4,1)} %bitcast), calls=%async_computation.3 | async-start | bytes 8388608
  65.8 30.7 %slice-start.1 = ((s8[8388608]{0:T(1024)(128)(4,1)}), s8[4194304]{0:T(1024)(128)(4,1)S(1)}, s32[]{:S(2)}) async-start(s8[8388608]{0:T(1024)(128)(4,1)} %bitcast), calls=%async_computation.4 | async-start | bytes 8388608
  65.8 30.6 %copy-start.6 = (bf16[4096,256]{1,0:T(8,128)(2,1)S(1)}, bf16[4096,256]{1,0:T(8,128)(2,1)}, u32[]{:S(2)}) copy-start(bf16[4096,256]{1,0:T(8,128)(2,1)} %refs_6_.1) | copy-start | bytes 6291460
  75.5 21.0 %copy-start.4 = (bf16[4096,256]{1,0:T(8,128)(2,1)S(1)}, bf16[4096,256]{1,0:T(8,128)(2,1)}, u32[]{:S(2)}) copy-start(bf16[4096,256]{1,0:T(8,128)(2,1)} %refs_5_.1) | copy-start | bytes 6291460
  75.5 2.7 %collective-permute-start.7 = (bf16[4,256,512]{2,1,0:T(8,128)(2,1)S(1)}, bf16[4,256,512]{2,1,0:T(8,128)(2,1)S(1)}, u32[]{:S(2)}, u32[]{:S(2)}) collective-permute-start(bf16[4,256,512]{2,1,0:T(8,128)(2,1)S(1)} %get-tuple-element.18), channel_id=1, source_target_pairs={{0,1},{1,0},{2,3},{3,2},{4,5},{5,4},{6,7},{7,6},{8,9},{9,8},{10,11... | collective-permute-start | bytes 3145736 | tf_op jit(solution)/shard_map/ppermute | solution.py:357
  78.5 9.2 %collective-permute-start.8 = (bf16[256,512]{1,0:T(8,128)(2,1)S(1)}, bf16[256,512]{1,0:T(8,128)(2,1)S(1)}, u32[]{:S(2)}, u32[]{:S(2)}) collective-permute-start(bf16[256,512]{1,0:T(8,128)(2,1)S(1)} %get-tuple-element.20), channel_id=1, source_target_pairs={{0,2},{1,3},{2,0},{3,1},{4,6},{5,7},{6,4},{7,5},{8,10},{9,11},{10,... | collective-permute-start | bytes 786440 | tf_op jit(solution)/shard_map/ppermute | solution.py:357
  80.0 14.6 %collective-permute-start.9 = (bf16[256,512]{1,0:T(8,128)(2,1)S(1)}, bf16[256,512]{1,0:T(8,128)(2,1)S(1)}, u32[]{:S(2)}, u32[]{:S(2)}) collective-permute-start(bf16[256,512]{1,0:T(8,128)(2,1)S(1)} %get-tuple-element.21), channel_id=1, source_target_pairs={{0,4},{1,5},{2,6},{3,7},{4,0},{5,1},{6,2},{7,3},{8,12},{9,13},{10,... | collective-permute-start | bytes 786440 | tf_op jit(solution)/shard_map/ppermute | solution.py:357
  83.1 13.3 %collective-permute-start.10 = (bf16[256,512]{1,0:T(8,128)(2,1)S(1)}, bf16[256,512]{1,0:T(8,128)(2,1)S(1)}, u32[]{:S(2)}, u32[]{:S(2)}) collective-permute-start(bf16[256,512]{1,0:T(8,128)(2,1)S(1)} %get-tuple-element.22), channel_id=1, source_target_pairs={{0,6},{1,7},{2,4},{3,5},{4,2},{5,3},{6,0},{7,1},{8,14},{9,15},{10,... | collective-permute-start | bytes 786440 | tf_op jit(solution)/shard_map/ppermute | solution.py:357
  101.6 1.3 copy-start.7
Sparse Core Ops, SparseCore 0:
  8.9 48.6 all-gather.1
  103.1 41.9 reduce-scatter.1

commit v2 on v1

v2 whole, which is shorter than its diff:
```python
import functools
import math

import jax
import jax.numpy as jnp
from jax import lax
from jax.experimental import pallas as pl
from jax.experimental.pallas import tpu as pltpu
from jax.sharding import PartitionSpec as P

ASKER_NUM = 32
SHARED_KV_NUM = 8
CHANNEL_DIM = 128

masked_score = -1e30
MIB = 1 << 20
VMEM = pltpu.VMEM


def mm(a, b):
    return lax.dot_general(a, b, (((1,), (0,)), ((), ())), preferred_element_type=jnp.float32)


def mm_nt(a, b):
    return lax.dot_general(a, b, (((1,), (1,)), ((), ())), preferred_element_type=jnp.float32)


def mm_tn(a, b):
    return lax.dot_general(a, b, (((0,), (0,)), ((), ())), preferred_element_type=jnp.float32)


def params():
    return pltpu.CompilerParams(vmem_limit_bytes=56 * MIB)


def cost(flops, moved):
    return pl.CostEstimate(flops=flops, bytes_accessed=moved, transcendentals=0)


def head_index():
    return lax.axis_index("head").astype(jnp.int32).reshape(1)


def upper_half(order):
    first = order[2 * lax.axis_index("ctx")]
    return jnp.where(2 * first >= order.shape[0], 0, 1)


def kv_body(x_ref, wk_ref, wv_ref, out_ref, acc):
    width = wk_ref.shape[1]
    step = pl.program_id(0)

    @pl.when(step == 0)
    def _():
        acc[...] = jnp.zeros_like(acc)

    x = x_ref[...]
    acc[:, :width] += mm(x, wk_ref[...])
    acc[:, width:] += mm(x, wv_ref[...])

    @pl.when(step == pl.num_programs(0) - 1)
    def _():
        out_ref[...] = acc[...].astype(out_ref.dtype)


def project_kv(x, wk, wv):
    tokens, depth = x.shape
    width = wk.shape[1]
    part = min(depth, 1024)
    return pl.pallas_call(
        kv_body,
        grid=(depth // part,),
        in_specs=[
            pl.BlockSpec((tokens, part), lambda i: (0, i)),
            pl.BlockSpec((part, width), lambda i: (i, 0)),
            pl.BlockSpec((part, width), lambda i: (i, 0)),
        ],
        out_specs=pl.BlockSpec((tokens, 2 * width), lambda i: (0, 0)),
        out_shape=jax.ShapeDtypeStruct((tokens, 2 * width), jnp.bfloat16),
        scratch_shapes=[VMEM((tokens, 2 * width), jnp.float32)],
        compiler_params=params(),
        cost_estimate=cost(4 * tokens * depth * width, 2 * depth * (tokens + 2 * width)),
        name="project_kv",
    )(x, wk, wv)


def project_body(x_ref, w_ref, out_ref):
    out_ref[...] = mm(x_ref[...], w_ref[...]).astype(out_ref.dtype)


def project(x, w):
    tokens, depth = x.shape
    width = w.shape[1]
    part = min(width, 256)
    return pl.pallas_call(
        project_body,
        grid=(width // part,),
        in_specs=[
            pl.BlockSpec((tokens, depth), lambda i: (0, 0)),
            pl.BlockSpec((depth, part), lambda i: (0, i)),
        ],
        out_specs=pl.BlockSpec((tokens, part), lambda i: (0, i)),
        out_shape=jax.ShapeDtypeStruct((tokens, width), jnp.bfloat16),
        compiler_params=params(),
        cost_estimate=cost(2 * tokens * depth * width, 2 * depth * (tokens + width)),
        name="project",
    )(x, w)


def split_body(order, x_ref, upper_ref, lower_ref):
    half = upper_ref.shape[0]
    at = upper_half(order) * half
    upper_ref[...] = x_ref[pl.ds(pl.multiple_of(at, half), half), :]
    lower_ref[...] = x_ref[pl.ds(pl.multiple_of(half - at, half), half), :]


def split_rows(x, span_order):
    tokens, width = x.shape
    return pl.pallas_call(
        split_body,
        in_specs=[pl.BlockSpec(memory_space=pltpu.SMEM), pl.BlockSpec(memory_space=VMEM)],
        out_specs=[pl.BlockSpec(memory_space=VMEM)] * 2,
        out_shape=[jax.ShapeDtypeStruct((tokens // 2, width), x.dtype)] * 2,
        compiler_params=params(),
        cost_estimate=cost(0, 4 * x.size),
        name="split_rows",
    )(span_order, x)


def back_body(*refs):
    w_ref, out_ref = refs[-2:]
    me = lax.axis_index("head")
    total = None
    for k, x_ref in enumerate(refs[:-2]):
        depth = x_ref.shape[1]
        at = pl.multiple_of((me ^ k) * depth, depth)
        term = mm_nt(x_ref[...], w_ref[:, pl.ds(at, depth)])
        total = term if total is None else total + term
    out_ref[...] = total.astype(out_ref.dtype)


def back_project(blocks, w):
    rows, depth = blocks[0].shape
    width = w.shape[0]
    part = min(width, 256)
    return pl.pallas_call(
        back_body,
        grid=(width // part,),
        in_specs=[pl.BlockSpec((rows, depth), lambda i: (0, 0))] * len(blocks)
        + [pl.BlockSpec((part, w.shape[1]), lambda i: (i, 0))],
        out_specs=pl.BlockSpec((rows, part), lambda i: (0, i)),
        out_shape=jax.ShapeDtypeStruct((rows, width), jnp.bfloat16),
        compiler_params=params(),
        cost_estimate=cost(2 * rows * w.size, 2 * w.size),
        name="back_project",
    )(*blocks, w)


def query_terms_body(me, dq_ref, w_ref, out_ref):
    out_ref[0] = mm_nt(dq_ref[...], w_ref[...])


def query_terms(dq, w, size):
    rows, depth = dq.shape
    share = w.shape[0] // size
    part = min(share, 512)
    count = share // part
    return pl.pallas_call(
        query_terms_body,
        grid_spec=pltpu.PrefetchScalarGridSpec(
            num_scalar_prefetch=1,
            grid=(size, count),
            in_specs=[
                pl.BlockSpec((rows, depth), lambda k, i, me: (0, 0)),
                pl.BlockSpec((part, depth), lambda k, i, me: ((me[0] ^ k) * count + i, 0)),
            ],
            out_specs=pl.BlockSpec((1, rows, part), lambda k, i, me: (k, 0, i)),
        ),
        out_shape=jax.ShapeDtypeStruct((size, rows, share), jnp.float32),
        compiler_params=params(),
        cost_estimate=cost(2 * rows * w.size, 2 * w.size + 4 * rows * w.shape[0]),
        name="query_terms",
    )(head_index(), dq, w)


def all_terms_body(count, me, first_ref, *refs):
    terms = refs[:count]
    wk_ref, wv_ref, out_ref, grads = refs[count:]
    width = wk_ref.shape[1]

    @pl.when((pl.program_id(0) == 0) & (pl.program_id(1) == 0))
    def _():
        total = terms[0][...].astype(jnp.float32)
        for term in terms[1:]:
            total = total + term[...].astype(jnp.float32)
        grads[...] = total.astype(grads.dtype)

    total = first_ref[0] + mm_nt(grads[:, :width], wk_ref[...])
    total = total + mm_nt(grads[:, width:], wv_ref[...])
    out_ref[0] = total.astype(out_ref.dtype)


def all_terms(first, terms, wk, wv):
    size, rows, share = first.shape
    width = wk.shape[1]
    part = min(share, 1024)
    count = share // part
    return pl.pallas_call(
        functools.partial(all_terms_body, len(terms)),
        grid_spec=pltpu.PrefetchScalarGridSpec(
            num_scalar_prefetch=1,
            grid=(size, count),
            in_specs=[pl.BlockSpec((1, rows, part), lambda k, i, me: (k, 0, i))]
            + [pl.BlockSpec((rows, 2 * width), lambda k, i, me: (0, 0))] * len(terms)
            + [pl.BlockSpec((part, width), lambda k, i, me: ((me[0] ^ k) * count + i, 0))] * 2,
            out_specs=pl.BlockSpec((1, rows, part), lambda k, i, me: (k, 0, i)),
            scratch_shapes=[VMEM((rows, 2 * width), jnp.bfloat16)],
        ),
        out_shape=jax.ShapeDtypeStruct((size, rows, share), jnp.bfloat16),
        compiler_params=params(),
        cost_estimate=cost(4 * rows * wk.size, 4 * wk.size + 6 * first.size),
        name="all_terms",
    )(head_index(), first, *terms, wk, wv)


def join_body(count, order, *refs):
    out_ref = refs[-1]
    half = refs[0].shape[0]
    at = upper_half(order) * half
    for j, place in enumerate((at, half - at)):
        total = refs[j * count][...].astype(jnp.float32)
        for ref in refs[j * count + 1 : (j + 1) * count]:
            total = total + ref[...].astype(jnp.float32)
        out_ref[pl.ds(pl.multiple_of(place, half), half), :] = total.astype(out_ref.dtype)


def join_rows(upper, lower, span_order):
    rows, width = upper[0].shape
    return pl.pallas_call(
        functools.partial(join_body, len(upper)),
        in_specs=[pl.BlockSpec(memory_space=pltpu.SMEM)]
        + [pl.BlockSpec(memory_space=VMEM)] * (2 * len(upper)),
        out_specs=pl.BlockSpec(memory_space=VMEM),
        out_shape=jax.ShapeDtypeStruct((2 * rows, width), jnp.bfloat16),
        compiler_params=params(),
        cost_estimate=cost(8 * rows * width, 20 * rows * width),
        name="join_rows",
    )(span_order, *upper, *lower)


def find_places(order, places, me, spans):
    for i in range(spans):
        places[order[i]] = ((i // 2) ^ me) * 2 + (i % 2)


def own_span(order, lengths, docs, me, j, half):
    span = order[2 * me + j]
    position = span * half + lax.broadcasted_iota(jnp.int32, (1, half), 1)
    first, end = 0, 0
    start = jnp.zeros((1, half), jnp.int32)
    for k in range(docs):
        end = end + lengths[k]
        start = jnp.where(position >= end, end, start)
        first = jnp.where(span * half >= end, end, first)
    return span, position, start, first // half


def stack_heads(ref, rows, group, share, dim):
    base = group * share
    return jnp.concatenate(
        [ref[rows, (base + h) * dim : (base + h + 1) * dim] for h in range(share)], axis=0
    )


def load_blocks(refs, held):
    rows = refs[0].shape[0]
    for k, ref in enumerate(refs):
        held[k * rows : (k + 1) * rows, :] = ref[...]


def allowed_of(p, position, start, half, share):
    key = p * half + lax.broadcasted_iota(jnp.int32, (half, 1), 0)
    allowed = (key <= position) & (key >= start)
    return jnp.concatenate([allowed] * share, axis=1)


def stats_body(sizes, order, lengths, q_ref, *refs):
    peers, half, groups, share, dim, docs = sizes
    blocks = refs[:peers]
    level_ref, mixed_ref, held, places = refs[peers:]
    me = lax.axis_index("ctx")
    width = groups * dim
    factor = math.log2(math.e) / math.sqrt(dim)
    find_places(order, places, me, 2 * peers)
    load_blocks(blocks, held)
    columns = share * half
    for j in range(2):
        span, position, start, lowest = own_span(order, lengths, docs, me, j, half)
        rows = slice(j * half, (j + 1) * half)
        queries = [stack_heads(q_ref, rows, g, share, dim) for g in range(groups)]

        def visit(p, carry):
            place = pl.multiple_of(places[p] * half, half)
            allowed = allowed_of(p, position, start, half, share)
            fresh = []
            for g in range(groups):
                top, total, mixed = carry[g]
                keys = held[pl.ds(place, half), g * dim : (g + 1) * dim]
                values = held[pl.ds(place, half), width + g * dim : width + (g + 1) * dim]
                logits = mm_nt(keys, queries[g]) * factor
                logits = jnp.where(allowed, logits, masked_score)
                higher = jnp.maximum(top, jnp.max(logits, axis=0, keepdims=True))
                weights = jnp.where(allowed, jnp.exp2(logits - higher), 0.0)
                fade = jnp.exp2(top - higher)
                total = total * fade + jnp.sum(weights, axis=0, keepdims=True)
                mixed = mixed * fade + mm_tn(values, weights.astype(jnp.bfloat16))
                fresh.append((higher, total, mixed))
            return tuple(fresh)

        empty = (
            jnp.full((1, columns), masked_score, jnp.float32),
            jnp.zeros((1, columns), jnp.float32),
            jnp.zeros((dim, columns), jnp.float32),
        )
        done = lax.fori_loop(lowest, span + 1, visit, (empty,) * groups)
        for g in range(groups):
            top, total, mixed = done[g]
            level_ref[j * groups + g] = top + jnp.log2(total)
            mixed_ref[j * groups + g] = mixed / total


def stats(q, blocks, span_order, doc_lengths, sizes):
    peers, half, groups, share, dim, docs = sizes
    columns = share * half
    return pl.pallas_call(
        functools.partial(stats_body, sizes),
        in_specs=[pl.BlockSpec(memory_space=pltpu.SMEM)] * 2
        + [pl.BlockSpec(memory_space=VMEM)] * (1 + peers),
        out_specs=[pl.BlockSpec(memory_space=VMEM)] * 2,
        out_shape=[
            jax.ShapeDtypeStruct((2 * groups, 1, columns), jnp.float32),
            jax.ShapeDtypeStruct((2 * groups, dim, columns), jnp.float32),
        ],
        scratch_shapes=[
            VMEM((2 * peers * half, 2 * groups * dim), jnp.bfloat16),
            pltpu.SMEM((2 * peers,), jnp.int32),
        ],
        compiler_params=params(),
        cost_estimate=cost(9 * peers * half * half * columns * groups * dim // dim, 6 * MIB),
        name="stats",
    )(span_order, doc_lengths, q, *blocks)


def grads_body(sizes, upper, order, lengths, q_ref, g_ref, level_ref, mixed_ref, *refs):
    peers, half, groups, share, dim, docs = sizes
    spans = 2 * peers
    if upper:
        blocks = refs[:peers]
        dq_ref, even_ref, odd_ref, rest_ref, held, sums, places = refs[peers:]
    else:
        rest_ref, blocks = refs[0], refs[1 : 1 + peers]
        dq_ref, even_ref, odd_ref, held, sums, places = refs[1 + peers :]
    me = lax.axis_index("ctx")
    width = groups * dim
    scale = 1.0 / math.sqrt(dim)
    factor = math.log2(math.e) * scale
    find_places(order, places, me, spans)
    load_blocks(blocks, held)
    columns = share * half
    at = upper_half(order)
    j = at if upper else 1 - at
    span, position, start, lowest = own_span(order, lengths, docs, me, j, half)
    if upper:
        sums[...] = jnp.zeros_like(sums)
    else:
        sums[...] = rest_ref[...]
    rows = pl.ds(pl.multiple_of(j * half, half), half)
    queries = [stack_heads(q_ref, rows, g, share, dim) for g in range(groups)]
    outs = [stack_heads(g_ref, slice(0, half), g, share, dim) for g in range(groups)]
    levels = [level_ref[j * groups + g] for g in range(groups)]
    deltas = []
    for g in range(groups):
        turned = jnp.concatenate(
            [outs[g][h * half : (h + 1) * half].astype(jnp.float32).T for h in range(share)],
            axis=1,
        )
        deltas.append(jnp.sum(turned * mixed_ref[j * groups + g], axis=0, keepdims=True))

    def visit(p, carry):
        place = pl.multiple_of(places[p] * half, half)
        target = pl.ds(pl.multiple_of(p * half, half), half)
        allowed = allowed_of(p, position, start, half, share)
        fresh = []
        for g in range(groups):
            keys = held[pl.ds(place, half), g * dim : (g + 1) * dim]
            values = held[pl.ds(place, half), width + g * dim : width + (g + 1) * dim]
            logits = mm_nt(keys, queries[g]) * factor
            chance = jnp.where(allowed, jnp.exp2(logits - levels[g]), 0.0)
            slopes = mm_nt(values, outs[g])
            score = (chance * (slopes - deltas[g])).astype(jnp.bfloat16)
            sums[target, g * dim : (g + 1) * dim] += mm(score, queries[g])
            sums[target, width + g * dim : width + (g + 1) * dim] += mm(
                chance.astype(jnp.bfloat16), outs[g]
            )
            fresh.append(carry[g] + mm_tn(keys, score))
        return tuple(fresh)

    empty = jnp.zeros((dim, columns), jnp.float32)
    done = lax.fori_loop(lowest, span + 1, visit, (empty,) * groups)
    for g in range(groups):
        for h in range(share):
            head = g * share + h
            dq_ref[:, head * dim : (head + 1) * dim] = (
                (done[g][:, h * half : (h + 1) * half].T * scale).astype(dq_ref.dtype)
            )
    for k in range(peers):
        out, slot = (even_ref, odd_ref)[k % 2], k // 2
        first = order[2 * (me ^ k)]
        other = spans - 1 - first
        pick = jnp.maximum(first, other) if upper else jnp.minimum(first, other)
        part = pl.ds(pl.multiple_of(pick * half, half), half)
        out[slot, :, :width] = (sums[part, :width] * scale).astype(out.dtype)
        out[slot, :, width:] = sums[part, width:].astype(out.dtype)
    if upper:
        rest_ref[...] = sums[: peers * half, :]


def grads(upper, q, g, level, mixed, rest, blocks, span_order, doc_lengths, sizes):
    peers, half, groups, share, dim, docs = sizes
    tokens, width = 2 * half, groups * dim
    columns = share * half
    terms = jax.ShapeDtypeStruct((peers // 2, half, 2 * width), jnp.bfloat16)
    rests = jax.ShapeDtypeStruct((peers * half, 2 * width), jnp.float32)
    outs = [jax.ShapeDtypeStruct(g.shape, jnp.bfloat16), terms, terms] + [rests] * upper
    return pl.pallas_call(
        functools.partial(grads_body, sizes, upper),
        in_specs=[pl.BlockSpec(memory_space=pltpu.SMEM)] * 2
        + [pl.BlockSpec(memory_space=VMEM)] * (4 + len(rest) + peers),
        out_specs=[pl.BlockSpec(memory_space=VMEM)] * len(outs),
        out_shape=outs,
        scratch_shapes=[
            VMEM((peers * tokens, 2 * width), jnp.bfloat16),
            VMEM(((2 if upper else 1) * peers * half, 2 * width), jnp.float32),
            pltpu.SMEM((2 * peers,), jnp.int32),
        ],
        compiler_params=params(),
        cost_estimate=cost((12 if upper else 6) * peers * half * half * columns * groups, 8 * MIB),
        name="upper_grads" if upper else "lower_grads",
    )(span_order, doc_lengths, q, g, level, mixed, *rest, *blocks)


def swap(x, k, axis):
    return lax.ppermute(x, axis, [(i, i ^ k) for i in range(lax.axis_size(axis))])


def gather_ctx(x):
    even = [x] + [swap(x, k, "ctx") for k in range(2, lax.axis_size("ctx"), 2)]
    odd = [swap(block, 1, "ctx") for block in even]
    return [block for pair in zip(even, odd) for block in pair]


def gather_head(x):
    return [x] + [swap(x, k, "head") for k in range(1, lax.axis_size("head"))]


def scatter_head(x):
    return [x[0]] + [swap(x[k], k, "head") for k in range(1, lax.axis_size("head"))]


def pair_body(even_ref, odd_ref, *outs):
    for k, out in enumerate(outs):
        out[...] = (
            even_ref[k].astype(jnp.float32) + odd_ref[k].astype(jnp.float32)
        ).astype(out.dtype)


def scatter_ctx(even, odd):
    count, rows, width = even.shape
    got = swap(odd, 1, "ctx")
    pairs = pl.pallas_call(
        pair_body,
        in_specs=[pl.BlockSpec(memory_space=VMEM)] * 2,
        out_specs=[pl.BlockSpec(memory_space=VMEM)] * count,
        out_shape=[jax.ShapeDtypeStruct((rows, width), jnp.bfloat16)] * count,
        compiler_params=params(),
        cost_estimate=cost(even.size, 6 * even.size),
        name="pair_sums",
    )(even, got)
    return [pairs[0]] + [swap(pairs[k], 2 * k, "ctx") for k in range(1, count)]


def shards(inputs, out_grad, w_query, w_key, value_projection, w_out, doc_lengths, span_order):
    tokens = inputs.shape[0]
    share = ASKER_NUM // SHARED_KV_NUM
    sizes = (
        lax.axis_size("ctx"),
        tokens // 2,
        w_key.shape[1] // CHANNEL_DIM,
        share,
        CHANNEL_DIM,
        doc_lengths.shape[0],
    )
    heads = lax.axis_size("head")
    upper_out, lower_out = split_rows(out_grad, span_order)
    upper_out = gather_head(upper_out)
    own = project_kv(inputs, w_key, value_projection)
    blocks = gather_ctx(own)
    query = project(inputs, w_query)
    level, mixed = stats(query, blocks, span_order, doc_lengths, sizes)
    upper_out, lower_out = lax.optimization_barrier((upper_out, lower_out))
    context_grad = back_project(upper_out, w_out)
    lower_out = gather_head(lower_out)
    query_grad, even, odd, rest = grads(
        True, query, context_grad, level, mixed, (), blocks, span_order, doc_lengths, sizes
    )
    first = query_terms(query_grad, w_query, heads)
    terms = scatter_ctx(even, odd)
    upper = scatter_head(all_terms(first, terms, w_key, value_projection))
    context_grad = back_project(lower_out, w_out)
    query_grad, even, odd = grads(
        False, query, context_grad, level, mixed, (rest,), blocks, span_order, doc_lengths, sizes
    )
    first = query_terms(query_grad, w_query, heads)
    terms = scatter_ctx(even, odd)
    lower = scatter_head(all_terms(first, terms, w_key, value_projection))
    return join_rows(upper, lower, span_order)


def solution(mesh):
    in_specs = (
        P("ctx", None),
        P("ctx", "head"),
        P(None, "head"),
        P(None, "head"),
        P(None, "head"),
        P("head", None),
        P(),
        P(),
    )
    out_specs = P("ctx", "head")
    return jax.shard_map(shards, mesh=mesh, in_specs=in_specs, out_specs=out_specs, check_vma=False)
```

time: 151 us -> 173 us (1.15); the launches traced: 152 us -> 171 us
  Pallas kernels: 31.7 us -> 89.9 us
  waiting for transfers between devices: 76.2 us -> 37.1 us
  starting transfers between devices: 11.1 us -> 33.1 us
  between operations: 13.7 us -> 0.23 us
  local copies, waits for them, and re-layouts: 19.1 us -> 10.8 us
    reduce_scatter x1 -> x0, waiting for transfers between devices: 42.1 us -> none  [shards(): lax.psum_scatter(partial_value, 'head', scatter_dimension=1, tiled=True)]
    pallas_call x2 -> x8, Pallas kernels: 14.8 us -> 50.1 us  [the longest x2 17.5 us: query_terms(): pl.pallas_call(query_terms_body, grid_spec=pltpu.PrefetchScalarGridSpec(n...]
    ppermute x11 -> x27, starting transfers between devices: 11.1 us -> 33.1 us  [swap(): lax.ppermute(x, axis, [(i, i ^ k) for i in range(lax.axis_size(axis))])]
    unnamed x60, local copies, waits for them, and re-layouts: 19.1 us -> 6.88 us
    ppermute x11 -> x27, waiting for transfers between devices: 26 us -> 37.1 us  [swap(): lax.ppermute(x, axis, [(i, i ^ k) for i in range(lax.axis_size(axis))])]
    pallas_call x1 -> x2, Pallas kernels: 3.07 us -> 13.5 us  [back_project(): pl.pallas_call(back_body, grid=(width // part,), in_specs=[pl.BlockSpec((...]
    all_gather x1 -> x0, waiting for transfers between devices: 7.34 us -> none  [shards(): gathered = lax.all_gather(out_grad, 'head', axis=1, tiled=True)]
    squeeze x0 -> x2, local copies, waits for them, and re-layouts: none -> 3.91 us  [scatter_head(): x[k]]
  transfers between devices with their start and end apart: 13 -> 27, of which waited for: 9 -> 7; matrix products, arithmetic and copies ran while one was open for 0% -> 2% of each run, Pallas kernels for 9% -> 42%
where the time goes in v2:
time: 173 us; the launch traced here: 171 us
  Pallas kernels  89.9 us (52%)
  waiting for transfers between devices  37.1 us (21%)
  starting transfers between devices  33.1 us (19%)
  local copies, waits for them, and re-layouts  10.8 us (6%)
    ppermute x27, waiting for transfers between devices, swap(): lax.ppermute(x, axis, [(i, i ^ k) for i in range(lax.axis_size(axis))])  37.1 us
    ppermute x27, starting transfers between devices, swap(): lax.ppermute(x, axis, [(i, i ^ k) for i in range(lax.axis_size(axis))])  33.1 us
    pallas_call x2, Pallas kernels, query_terms(): pl.pallas_call(query_terms_body, grid_spec=pltpu.PrefetchScalarGridSpec(n...  17.5 us
    pallas_call x2, Pallas kernels, grads(): pl.pallas_call(functools.partial(grads_body, sizes, upper), in_specs=[pl....  16.9 us
    pallas_call x2, Pallas kernels, back_project(): pl.pallas_call(back_body, grid=(width // part,), in_specs=[pl.BlockSpec((...  13.5 us
    pallas_call x2, Pallas kernels, all_terms(): pl.pallas_call(functools.partial(all_terms_body, len(terms)), grid_spec=p...  11.2 us
    pallas_call x1, Pallas kernels, stats(): pl.pallas_call(functools.partial(stats_body, sizes), in_specs=[pl.BlockSp...  10.4 us
    unnamed x60, local copies, waits for them, and re-layouts  6.88 us
  transfers between devices with their start and end apart: 27, of which 7 were waited for; matrix products, arithmetic and copies ran while one was open for 2% of the time, Pallas kernels for 42%

profile of v2, /device:TPU:0, one launch (start us, length us, event | category | flops | bytes accessed | tf_op | source)
XLA Modules:
  0.0 171.1 jit_solution(1779798716693498698)
XLA Ops:
  0.0 1.9 %split_rows.1 = (bf16[128,1024]{1,0:T(8,128)(2,1)}, bf16[128,1024]{1,0:T(8,128)(2,1)}) custom-call(s32[16]{0:T(128)} %order.9, bf16[256,1024]{1,0:T(8,128)(2,1)} %x_ref.4), custom_call_target="tpu_custom_call" | custom-call | bytes 1048576 | tf_op jit(solution)/shard_map/split_rows/pallas_call | solution.py:119
  2.0 3.0 %collective-permute-start = (bf16[128,1024]{1,0:T(8,128)(2,1)}, bf16[128,1024]{1,0:T(8,128)(2,1)S(1)}, u32[]{:S(2)}, u32[]{:S(2)}) collective-permute-start(bf16[128,1024]{1,0:T(8,128)(2,1)} %get-tuple-element.31.refs_0_), channel_id=1, source_target_pairs={{0,8},{8,0},{16,24},{24,16},{1,9},{9,1},{17,25},{25,17},{2,10},{10... | collective-permute-start | bytes 786440 | tf_op jit(solution)/shard_map/ppermute | solution.py:453
  5.0 2.6 %collective-permute-start.1 = (bf16[128,1024]{1,0:T(8,128)(2,1)}, bf16[128,1024]{1,0:T(8,128)(2,1)S(1)}, u32[]{:S(2)}, u32[]{:S(2)}) collective-permute-start(bf16[128,1024]{1,0:T(8,128)(2,1)} %get-tuple-element.31.refs_0_), channel_id=1, source_target_pairs={{0,16},{8,24},{16,0},{24,8},{1,17},{9,25},{17,1},{25,9},{2,18},{10... | collective-permute-start | bytes 786440 | tf_op jit(solution)/shard_map/ppermute | solution.py:453
  7.6 4.9 %project_kv.1.refs_0_.refs_1_ = bf16[256,512]{1,0:T(8,128)(2,1)} custom-call(bf16[256,4096]{1,0:T(8,128)(2,1)} %x_ref.5, bf16[4096,256]{1,0:T(8,128)(2,1)} %refs_4_.7, bf16[4096,256]{1,0:T(8,128)(2,1)} %refs_5_.3), custom_call_target="tpu_custom_call" | custom-call | flops 1073741824 | bytes 6291456 | tf_op jit(solution)/shard_map/project_kv/pallas_call | solution.py:70
  12.5 1.5 collective-permute-start.4
  14.0 1.5 collective-permute-start.6
  16.0 1.0 collective-permute-done.refs_1_
  17.1 2.6 %collective-permute-start.2 = (bf16[128,1024]{1,0:T(8,128)(2,1)S(1)}, bf16[128,1024]{1,0:T(8,128)(2,1)S(1)}, u32[]{:S(2)}, u32[]{:S(2)}) collective-permute-start(bf16[128,1024]{1,0:T(8,128)(2,1)S(1)} %copy-done.10), channel_id=1, source_target_pairs={{0,24},{8,16},{16,8},{24,0},{1,25},{9,17},{17,9},{25,1},{2,26},{10... | collective-permute-start | bytes 786440 | tf_op jit(solution)/shard_map/ppermute | solution.py:453
  19.7 2.3 %collective-permute-done.4.refs_2_.refs_3_ = bf16[256,512]{1,0:T(8,128)(2,1)S(1)} collective-permute-done((bf16[256,512]{1,0:T(8,128)(2,1)}, bf16[256,512]{1,0:T(8,128)(2,1)S(1)}, u32[]{:S(2)}, u32[]{:S(2)}) %collective-permute-start.4) | collective-permute-done | bytes 262176 | tf_op jit(solution)/shard_map/ppermute | solution.py:453
  22.0 5.1 %collective-permute-done.6.refs_4_.refs_5_ = bf16[256,512]{1,0:T(8,128)(2,1)S(1)} collective-permute-done((bf16[256,512]{1,0:T(8,128)(2,1)}, bf16[256,512]{1,0:T(8,128)(2,1)S(1)}, u32[]{:S(2)}, u32[]{:S(2)}) %collective-permute-start.6) | collective-permute-done | bytes 262176 | tf_op jit(solution)/shard_map/ppermute | solution.py:453
  27.6 6.8 %project.1.q_ref = bf16[256,1024]{1,0:T(8,128)(2,1)} custom-call(bf16[256,4096]{1,0:T(8,128)(2,1)} %x_ref.5, bf16[4096,1024]{1,0:T(8,128)(2,1)} %w_ref.5), custom_call_target="tpu_custom_call" | custom-call | flops 2147483648 | bytes 10485760 | tf_op jit(solution)/shard_map/project/pallas_call | solution.py:95
  35.2 6.7 %back_project.2.g_ref = bf16[128,1024]{1,0:T(8,128)(2,1)} custom-call(bf16[128,1024]{1,0:T(8,128)(2,1)} %get-tuple-element.31.refs_0_, bf16[128,1024]{1,0:T(8,128)(2,1)} %copy-done.11, bf16[128,1024]{1,0:T(8,128)(2,1)} %copy-done.12, bf16[128,1024]{1,0:T(8,128)(2,1)} %copy-done.14, bf16[1024,4096]{1,0:T(8,128)(2,1)} %refs_4_.6), custom_call_target="tpu_custom_call" | custom-call | flops 1073741824 | bytes 8388608 | tf_op jit(solution)/shard_map/back_project/pallas_call | solution.py:146
  41.9 2.3 %collective-permute-start.18 = (bf16[128,1024]{1,0:T(8,128)(2,1)S(1)}, bf16[128,1024]{1,0:T(8,128)(2,1)S(1)}, u32[]{:S(2)}, u32[]{:S(2)}) collective-permute-start(bf16[128,1024]{1,0:T(8,128)(2,1)S(1)} %copy-done.2), channel_id=1, source_target_pairs={{0,16},{8,24},{16,0},{24,8},{1,17},{9,25},{17,1},{25,9},{2,18},{10... | collective-permute-start | bytes 786440 | tf_op jit(solution)/shard_map/ppermute | solution.py:453
  44.2 1.6 collective-permute-start.19
  45.8 0.7 copy-done.8
  46.5 0.7 copy-done.9
  47.2 10.4 %stats.1 = (f32[4,1,512]{2,1,0:T(1,128)}, f32[4,128,512]{2,1,0:T(8,128)}) custom-call(s32[16]{0:T(128)} %order.9, s32[8]{0:T(128)} %lengths.5, bf16[256,1024]{1,0:T(8,128)(2,1)} %project.1.q_ref, bf16[256,512]{1,0:T(8,128)(2,1)} %project_kv.1.refs_0_.refs_1_, bf16[256,512]{1,0:T(8,128)(2,1)} %copy-done.6, bf16[256,512]{1,0:T(8,128)(2,1)} %copy-done.3, ...), custom_call_target="tpu_custom_call" | custom-call | flops 1207959552 | bytes 6291456 | tf_op jit(solution)/shard_map/stats/pallas_call | solution.py:335
  57.6 10.8 %upper_grads.1 = (bf16[128,1024]{1,0:T(8,128)(2,1)}, bf16[4,128,512]{2,1,0:T(8,128)(2,1)}, bf16[4,128,512]{2,1,0:T(8,128)(2,1)}, f32[1024,512]{1,0:T(8,128)}) custom-call(s32[16]{0:T(128)} %order.9, s32[8]{0:T(128)} %lengths.5, bf16[256,1024]{1,0:T(8,128)(2,1)} %project.1.q_ref, bf16[128,1024]{1,0:T(8,128)(2,1)} %back_project.2.g_ref, ...), custom_call_target="tpu_custom_call" | custom-call | flops 1610612736 | bytes 8388608 | tf_op jit(solution)/shard_map/upper_grads/pallas_call | solution.py:435
  68.5 0.7 copy-done.13
  69.3 0.7 copy-done.16
  70.0 6.8 %back_project.3.g_ref = bf16[128,1024]{1,0:T(8,128)(2,1)} custom-call(bf16[128,1024]{1,0:T(8,128)(2,1)} %get-tuple-element.44.refs_0_, bf16[128,1024]{1,0:T(8,128)(2,1)} %copy-done.13, bf16[128,1024]{1,0:T(8,128)(2,1)} %copy-done.15, bf16[128,1024]{1,0:T(8,128)(2,1)} %copy-done.16, bf16[1024,4096]{1,0:T(8,128)(2,1)} %refs_4_.6), custom_call_target="tpu_custom_call" | custom-call | flops 1073741824 | bytes 8388608 | tf_op jit(solution)/shard_map/back_project/pallas_call | solution.py:146
  76.8 6.1 %lower_grads.1 = (bf16[128,1024]{1,0:T(8,128)(2,1)}, bf16[4,128,512]{2,1,0:T(8,128)(2,1)}, bf16[4,128,512]{2,1,0:T(8,128)(2,1)}) custom-call(s32[16]{0:T(128)} %order.9, s32[8]{0:T(128)} %lengths.5, bf16[256,1024]{1,0:T(8,128)(2,1)} %project.1.q_ref, bf16[128,1024]{1,0:T(8,128)(2,1)} %back_project.3.g_ref, f32[4,1,512]{2,1,0:T(1,128)} %get-tuple-element.35.level_ref, ...), custom_call_target="tpu_custom_call" | custom-call | flops 805306368 | bytes 8388608 | tf_op jit(solution)/shard_map/lower_grads/pallas_call | solution.py:435
  82.8 0.8 collective-permute-start.20
  83.7 1.7 collective-permute-done.20.odd_ref
  85.3 0.8 copy-done.1
  86.1 2.0 %pair_sums.3 = (bf16[128,512]{1,0:T(8,128)(2,1)}, bf16[128,512]{1,0:T(8,128)(2,1)}, bf16[128,512]{1,0:T(8,128)(2,1)}, bf16[128,512]{1,0:T(8,128)(2,1)}) custom-call(bf16[4,128,512]{2,1,0:T(8,128)(2,1)} %get-tuple-element.47.even_ref, bf16[4,128,512]{2,1,0:T(8,128)(2,1)} %copy-done.1), custom_call_target="tpu_custom_call" | custom-call | flops 262144 | bytes 1572864 | tf_op jit(solution)/shard_map/pair_sums/pallas_call | solution.py:480
  88.4 3.3 %collective-permute-start.23 = (bf16[128,512]{1,0:T(8,128)(2,1)}, bf16[128,512]{1,0:T(8,128)(2,1)S(1)}, u32[]{:S(2)}, u32[]{:S(2)}) collective-permute-start(bf16[128,512]{1,0:T(8,128)(2,1)} %get-tuple-element.52), channel_id=1, source_target_pairs={{0,6},{1,7},{2,4},{3,5},{4,2},{5,3},{6,0},{7,1},{8,14},{9,15},{10,... | collective-permute-start | bytes 393224 | tf_op jit(solution)/shard_map/ppermute | solution.py:453
  91.7 8.8 %query_terms.3.first_ref = f32[4,128,1024]{2,1,0:T(8,128)} custom-call(s32[1]{0:T(128)} %bitcast.me, bf16[128,1024]{1,0:T(8,128)(2,1)} %get-tuple-element.46.dq_ref, bf16[4096,1024]{1,0:T(8,128)(2,1)} %w_ref.5), custom_call_target="tpu_custom_call" | custom-call | flops 1073741824 | bytes 10485760 | tf_op jit(solution)/shard_map/query_terms/pallas_call | solution.py:168
  100.5 8.8 %query_terms.2.first_ref = f32[4,128,1024]{2,1,0:T(8,128)} custom-call(s32[1]{0:T(128)} %bitcast.me, bf16[128,1024]{1,0:T(8,128)(2,1)} %get-tuple-element.37.dq_ref, bf16[4096,1024]{1,0:T(8,128)(2,1)} %w_ref.5), custom_call_target="tpu_custom_call" | custom-call | flops 1073741824 | bytes 10485760 | tf_op jit(solution)/shard_map/query_terms/pallas_call | solution.py:168
  109.2 0.8 copy-done
  110.0 2.0 %pair_sums.2 = (bf16[128,512]{1,0:T(8,128)(2,1)}, bf16[128,512]{1,0:T(8,128)(2,1)}, bf16[128,512]{1,0:T(8,128)(2,1)}, bf16[128,512]{1,0:T(8,128)(2,1)}) custom-call(bf16[4,128,512]{2,1,0:T(8,128)(2,1)} %get-tuple-element.38.even_ref, bf16[4,128,512]{2,1,0:T(8,128)(2,1)} %copy-done), custom_call_target="tpu_custom_call" | custom-call | flops 262144 | bytes 1572864 | tf_op jit(solution)/shard_map/pair_sums/pallas_call | solution.py:480
  112.1 0.6 collective-permute-start.12
  112.6 2.9 %collective-permute-start.13 = (bf16[128,512]{1,0:T(8,128)(2,1)}, bf16[128,512]{1,0:T(8,128)(2,1)S(1)}, u32[]{:S(2)}, u32[]{:S(2)}) collective-permute-start(bf16[128,512]{1,0:T(8,128)(2,1)} %get-tuple-element.43), channel_id=1, source_target_pairs={{0,6},{1,7},{2,4},{3,5},{4,2},{5,3},{6,0},{7,1},{8,14},{9,15},{10,... | collective-permute-start | bytes 393224 | tf_op jit(solution)/shard_map/ppermute | solution.py:453
  115.6 0.6 copy-done.27
  116.3 5.6 %all_terms.3 = bf16[4,128,1024]{2,1,0:T(8,128)(2,1)} custom-call(s32[1]{0:T(128)} %bitcast.me, f32[4,128,1024]{2,1,0:T(8,128)} %query_terms.3.first_ref, bf16[128,512]{1,0:T(8,128)(2,1)} %get-tuple-element.49.refs_0_, bf16[128,512]{1,0:T(8,128)(2,1)} %copy-done.25, bf16[128,512]{1,0:T(8,128)(2,1)} %copy-done.27, bf16[128,512]{1,0:T(8,128)(2,1)} %copy-done.28, ...), custom_call_target="tpu_custom_call" | custom-call | flops 536870912 | bytes 7340032 | tf_op jit(solution)/shard_map/all_terms/pallas_call | solution.py:208
  121.9 1.9 %slice_bitcast_fusion = (bf16[128,1024]{1,0:T(8,128)(2,1)S(1)}, bf16[128,1024]{1,0:T(8,128)(2,1)S(1)}, bf16[128,1024]{1,0:T(8,128)(2,1)S(1)}, bf16[128,1024]{1,0:T(8,128)(2,1)}) fusion(bf16[4,128,1024]{2,1,0:T(8,128)(2,1)} %all_terms.3), kind=kLoop, calls=%fused_computation | loop fusion | bytes 2097152 | tf_op jit(solution)/shard_map/squeeze | solution.py:467
  123.9 2.8 %collective-permute-start.25 = (bf16[128,1024]{1,0:T(8,128)(2,1)S(1)}, bf16[128,1024]{1,0:T(8,128)(2,1)S(1)}, u32[]{:S(2)}, u32[]{:S(2)}) collective-permute-start(bf16[128,1024]{1,0:T(8,128)(2,1)S(1)} %get-tuple-element.54), channel_id=1, source_target_pairs={{0,16},{8,24},{16,0},{24,8},{1,17},{9,25},{17,1},{25,9},{2,18},{10... | collective-permute-start | bytes 786440 | tf_op jit(solution)/shard_map/ppermute | solution.py:453
  126.6 1.6 collective-permute-start.26
  128.2 0.6 copy-done.24
  128.9 5.6 %all_terms.2 = bf16[4,128,1024]{2,1,0:T(8,128)(2,1)} custom-call(s32[1]{0:T(128)} %bitcast.me, f32[4,128,1024]{2,1,0:T(8,128)} %query_terms.2.first_ref, bf16[128,512]{1,0:T(8,128)(2,1)} %get-tuple-element.40.refs_0_, bf16[128,512]{1,0:T(8,128)(2,1)} %copy-done.23, bf16[128,512]{1,0:T(8,128)(2,1)} %copy-done.24, bf16[128,512]{1,0:T(8,128)(2,1)} %copy-done.26, ...), custom_call_target="tpu_custom_call" | custom-call | flops 536870912 | bytes 7340032 | tf_op jit(solution)/shard_map/all_terms/pallas_call | solution.py:208
  134.5 2.0 %slice_bitcast_fusion.4 = (bf16[128,1024]{1,0:T(8,128)(2,1)S(1)}, bf16[128,1024]{1,0:T(8,128)(2,1)S(1)}, bf16[128,1024]{1,0:T(8,128)(2,1)S(1)}, bf16[128,1024]{1,0:T(8,128)(2,1)}) fusion(bf16[4,128,1024]{2,1,0:T(8,128)(2,1)} %all_terms.2), kind=kLoop, calls=%fused_computation.4 | loop fusion | bytes 2097152 | tf_op jit(solution)/shard_map/squeeze | solution.py:467
  136.4 2.8 %collective-permute-start.15 = (bf16[128,1024]{1,0:T(8,128)(2,1)S(1)}, bf16[128,1024]{1,0:T(8,128)(2,1)S(1)}, u32[]{:S(2)}, u32[]{:S(2)}) collective-permute-start(bf16[128,1024]{1,0:T(8,128)(2,1)S(1)} %get-tuple-element.58), channel_id=1, source_target_pairs={{0,16},{8,24},{16,0},{24,8},{1,17},{9,25},{17,1},{25,9},{2,18},{10... | collective-permute-start | bytes 786440 | tf_op jit(solution)/shard_map/ppermute | solution.py:453
  139.3 1.6 collective-permute-start.16
  140.8 4.5 %collective-permute-done.25.refs_6_ = bf16[128,1024]{1,0:T(8,128)(2,1)S(1)} collective-permute-done((bf16[128,1024]{1,0:T(8,128)(2,1)S(1)}, bf16[128,1024]{1,0:T(8,128)(2,1)S(1)}, u32[]{:S(2)}, u32[]{:S(2)}) %collective-permute-start.25) | collective-permute-done | bytes 262176 | tf_op jit(solution)/shard_map/ppermute | solution.py:453
  145.3 3.8 %collective-permute-done.14.refs_1_ = bf16[128,1024]{1,0:T(8,128)(2,1)S(1)} collective-permute-done((bf16[128,1024]{1,0:T(8,128)(2,1)S(1)}, bf16[128,1024]{1,0:T(8,128)(2,1)S(1)}, u32[]{:S(2)}, u32[]{:S(2)}) %collective-permute-start.14) | collective-permute-done | bytes 262176 | tf_op jit(solution)/shard_map/ppermute | solution.py:453
  149.1 18.6 %collective-permute-done.15.refs_2_ = bf16[128,1024]{1,0:T(8,128)(2,1)S(1)} collective-permute-done((bf16[128,1024]{1,0:T(8,128)(2,1)S(1)}, bf16[128,1024]{1,0:T(8,128)(2,1)S(1)}, u32[]{:S(2)}, u32[]{:S(2)}) %collective-permute-start.15) | collective-permute-done | bytes 262176 | tf_op jit(solution)/shard_map/ppermute | solution.py:453
  167.8 0.7 copy-done.21
  168.6 2.6 %join_rows.1 = bf16[256,1024]{1,0:T(8,128)(2,1)} custom-call(s32[16]{0:T(128)} %order.9, bf16[128,1024]{1,0:T(8,128)(2,1)} %get-tuple-element.60.refs_0_, bf16[128,1024]{1,0:T(8,128)(2,1)} %copy-done.20, bf16[128,1024]{1,0:T(8,128)(2,1)} %copy-done.21, bf16[128,1024]{1,0:T(8,128)(2,1)} %copy-done.22, bf16[128,1024]{1,0:T(8,128)(2,1)} %get-tuple-element.56.refs_4_, ...), custom_call_target="tpu_custom_call" | custom-call | flops 1048576 | bytes 2621440 | tf_op jit(solution)/shard_map/join_rows/pallas_call | solution.py:239
  (83 shorter events, 2.4 us)
Async XLA Ops:
  1.9 15.1 %copy-start.10 = (bf16[128,1024]{1,0:T(8,128)(2,1)S(1)}, bf16[128,1024]{1,0:T(8,128)(2,1)}, u32[]{:S(2)}) copy-start(bf16[128,1024]{1,0:T(8,128)(2,1)} %get-tuple-element.31.refs_0_) | copy-start | bytes 786436
  2.0 15.1 %collective-permute-start = (bf16[128,1024]{1,0:T(8,128)(2,1)}, bf16[128,1024]{1,0:T(8,128)(2,1)S(1)}, u32[]{:S(2)}, u32[]{:S(2)}) collective-permute-start(bf16[128,1024]{1,0:T(8,128)(2,1)} %get-tuple-element.31.refs_0_), channel_id=1, source_target_pairs={{0,8},{8,0},{16,24},{24,16},{1,9},{9,1},{17,25},{25,17},{2,10},{10... | collective-permute-start | bytes 786440 | tf_op jit(solution)/shard_map/ppermute | solution.py:453
  5.0 14.7 %collective-permute-start.1 = (bf16[128,1024]{1,0:T(8,128)(2,1)}, bf16[128,1024]{1,0:T(8,128)(2,1)S(1)}, u32[]{:S(2)}, u32[]{:S(2)}) collective-permute-start(bf16[128,1024]{1,0:T(8,128)(2,1)} %get-tuple-element.31.refs_0_), channel_id=1, source_target_pairs={{0,16},{8,24},{16,0},{24,8},{1,17},{9,25},{17,1},{25,9},{2,18},{10... | collective-permute-start | bytes 786440 | tf_op jit(solution)/shard_map/ppermute | solution.py:453
  12.5 21.9 %copy-start.2 = (bf16[128,1024]{1,0:T(8,128)(2,1)S(1)}, bf16[128,1024]{1,0:T(8,128)(2,1)}, u32[]{:S(2)}) copy-start(bf16[128,1024]{1,0:T(8,128)(2,1)} %get-tuple-element.44.refs_0_) | copy-start | bytes 786436
  12.5 9.5 %collective-permute-start.4 = (bf16[256,512]{1,0:T(8,128)(2,1)}, bf16[256,512]{1,0:T(8,128)(2,1)S(1)}, u32[]{:S(2)}, u32[]{:S(2)}) collective-permute-start(bf16[256,512]{1,0:T(8,128)(2,1)} %project_kv.1.refs_0_.refs_1_), channel_id=1, source_target_pairs={{0,2},{1,3},{2,0},{3,1},{4,6},{5,7},{6,4},{7,5},{8,10},{9,11},{10,... | collective-permute-start | bytes 786440 | tf_op jit(solution)/shard_map/ppermute | solution.py:453
  14.0 13.0 %collective-permute-start.6 = (bf16[256,512]{1,0:T(8,128)(2,1)}, bf16[256,512]{1,0:T(8,128)(2,1)S(1)}, u32[]{:S(2)}, u32[]{:S(2)}) collective-permute-start(bf16[256,512]{1,0:T(8,128)(2,1)} %project_kv.1.refs_0_.refs_1_), channel_id=1, source_target_pairs={{0,4},{1,5},{2,6},{3,7},{4,0},{5,1},{6,2},{7,3},{8,12},{9,13},{10,... | collective-permute-start | bytes 786440 | tf_op jit(solution)/shard_map/ppermute | solution.py:453
  15.5 11.5 %collective-permute-start.8 = (bf16[256,512]{1,0:T(8,128)(2,1)}, bf16[256,512]{1,0:T(8,128)(2,1)S(1)}, u32[]{:S(2)}, u32[]{:S(2)}) collective-permute-start(bf16[256,512]{1,0:T(8,128)(2,1)} %project_kv.1.refs_0_.refs_1_), channel_id=1, source_target_pairs={{0,6},{1,7},{2,4},{3,5},{4,2},{5,3},{6,0},{7,1},{8,14},{9,15},{10,... | collective-permute-start | bytes 786440 | tf_op jit(solution)/shard_map/ppermute | solution.py:453
  17.0 17.4 %copy-start.11 = (bf16[128,1024]{1,0:T(8,128)(2,1)}, bf16[128,1024]{1,0:T(8,128)(2,1)S(1)}, u32[]{:S(2)}) copy-start(bf16[128,1024]{1,0:T(8,128)(2,1)S(1)} %collective-permute-done.refs_1_) | copy-start | bytes 786436
  17.1 17.4 %collective-permute-start.2 = (bf16[128,1024]{1,0:T(8,128)(2,1)S(1)}, bf16[128,1024]{1,0:T(8,128)(2,1)S(1)}, u32[]{:S(2)}, u32[]{:S(2)}) collective-permute-start(bf16[128,1024]{1,0:T(8,128)(2,1)S(1)} %copy-done.10), channel_id=1, source_target_pairs={{0,24},{8,16},{16,8},{24,0},{1,25},{9,17},{17,9},{25,1},{2,26},{10... | collective-permute-start | bytes 786440 | tf_op jit(solution)/shard_map/ppermute | solution.py:453
  19.6 14.8 %copy-start.12 = (bf16[128,1024]{1,0:T(8,128)(2,1)}, bf16[128,1024]{1,0:T(8,128)(2,1)S(1)}, u32[]{:S(2)}) copy-start(bf16[128,1024]{1,0:T(8,128)(2,1)S(1)} %collective-permute-done.1.refs_2_) | copy-start | bytes 786436
  19.6 22.3 %collective-permute-start.3 = (bf16[256,512]{1,0:T(8,128)(2,1)}, bf16[256,512]{1,0:T(8,128)(2,1)S(1)}, u32[]{:S(2)}, u32[]{:S(2)}) collective-permute-start(bf16[256,512]{1,0:T(8,128)(2,1)} %project_kv.1.refs_0_.refs_1_), channel_id=1, source_target_pairs={{0,1},{1,0},{2,3},{3,2},{4,5},{5,4},{6,7},{7,6},{8,9},{9,8},{10,11... | collective-permute-start | bytes 786440 | tf_op jit(solution)/shard_map/ppermute | solution.py:453
  22.0 12.4 %copy-start.3 = (bf16[256,512]{1,0:T(8,128)(2,1)}, bf16[256,512]{1,0:T(8,128)(2,1)S(1)}, u32[]{:S(2)}) copy-start(bf16[256,512]{1,0:T(8,128)(2,1)S(1)} %collective-permute-done.4.refs_2_.refs_3_) | copy-start | bytes 786436
  22.0 22.2 %collective-permute-start.5 = (bf16[256,512]{1,0:T(8,128)(2,1)S(1)}, bf16[256,512]{1,0:T(8,128)(2,1)S(1)}, u32[]{:S(2)}, u32[]{:S(2)}) collective-permute-start(bf16[256,512]{1,0:T(8,128)(2,1)S(1)} %collective-permute-done.4.refs_2_.refs_3_), channel_id=1, source_target_pairs={{0,1},{1,0},{2,3},{3,2},{4,5},{5,4},{6,7},{7,6},{8,9},{9,8},{10,11... | collective-permute-start | bytes 786440 | tf_op jit(solution)/shard_map/ppermute | solution.py:453
  27.0 7.4 %copy-start.4 = (bf16[256,512]{1,0:T(8,128)(2,1)}, bf16[256,512]{1,0:T(8,128)(2,1)S(1)}, u32[]{:S(2)}) copy-start(bf16[256,512]{1,0:T(8,128)(2,1)S(1)} %collective-permute-done.6.refs_4_.refs_5_) | copy-start | bytes 786436
  27.0 18.7 %collective-permute-start.7 = (bf16[256,512]{1,0:T(8,128)(2,1)S(1)}, bf16[256,512]{1,0:T(8,128)(2,1)S(1)}, u32[]{:S(2)}, u32[]{:S(2)}) collective-permute-start(bf16[256,512]{1,0:T(8,128)(2,1)S(1)} %collective-permute-done.6.refs_4_.refs_5_), channel_id=1, source_target_pairs={{0,1},{1,0},{2,3},{3,2},{4,5},{5,4},{6,7},{7,6},{8,9},{9,8},{10,11... | collective-permute-start | bytes 786440 | tf_op jit(solution)/shard_map/ppermute | solution.py:453
  27.1 7.4 %copy-start.5 = (bf16[256,512]{1,0:T(8,128)(2,1)}, bf16[256,512]{1,0:T(8,128)(2,1)S(1)}, u32[]{:S(2)}) copy-start(bf16[256,512]{1,0:T(8,128)(2,1)S(1)} %collective-permute-done.8.refs_6_.refs_7_) | copy-start | bytes 786436
  27.1 18.7 %collective-permute-start.9 = (bf16[256,512]{1,0:T(8,128)(2,1)S(1)}, bf16[256,512]{1,0:T(8,128)(2,1)S(1)}, u32[]{:S(2)}, u32[]{:S(2)}) collective-permute-start(bf16[256,512]{1,0:T(8,128)(2,1)S(1)} %collective-permute-done.8.refs_6_.refs_7_), channel_id=1, source_target_pairs={{0,1},{1,0},{2,3},{3,2},{4,5},{5,4},{6,7},{7,6},{8,9},{9,8},{10,11... | collective-permute-start | bytes 786440 | tf_op jit(solution)/shard_map/ppermute | solution.py:453
  34.5 34.0 %collective-permute-start.17 = (bf16[128,1024]{1,0:T(8,128)(2,1)S(1)}, bf16[128,1024]{1,0:T(8,128)(2,1)S(1)}, u32[]{:S(2)}, u32[]{:S(2)}) collective-permute-start(bf16[128,1024]{1,0:T(8,128)(2,1)S(1)} %copy-done.2), channel_id=1, source_target_pairs={{0,8},{8,0},{16,24},{24,16},{1,9},{9,1},{17,25},{25,17},{2,10},{10... | collective-permute-start | bytes 786440 | tf_op jit(solution)/shard_map/ppermute | solution.py:453
  41.9 3.8 %copy-start.6 = (bf16[256,512]{1,0:T(8,128)(2,1)}, bf16[256,512]{1,0:T(8,128)(2,1)S(1)}, u32[]{:S(2)}) copy-start(bf16[256,512]{1,0:T(8,128)(2,1)S(1)} %collective-permute-done.3.refs_1_.refs_2_) | copy-start | bytes 786436
  41.9 26.6 %collective-permute-start.18 = (bf16[128,1024]{1,0:T(8,128)(2,1)S(1)}, bf16[128,1024]{1,0:T(8,128)(2,1)S(1)}, u32[]{:S(2)}, u32[]{:S(2)}) collective-permute-start(bf16[128,1024]{1,0:T(8,128)(2,1)S(1)} %copy-done.2), channel_id=1, source_target_pairs={{0,16},{8,24},{16,0},{24,8},{1,17},{9,25},{17,1},{25,9},{2,18},{10... | collective-permute-start | bytes 786440 | tf_op jit(solution)/shard_map/ppermute | solution.py:453
  44.2 1.6 copy-start.7
  44.2 24.3 %collective-permute-start.19 = (bf16[128,1024]{1,0:T(8,128)(2,1)S(1)}, bf16[128,1024]{1,0:T(8,128)(2,1)S(1)}, u32[]{:S(2)}, u32[]{:S(2)}) collective-permute-start(bf16[128,1024]{1,0:T(8,128)(2,1)S(1)} %copy-done.2), channel_id=1, source_target_pairs={{0,24},{8,16},{16,8},{24,0},{1,25},{9,17},{17,9},{25,1},{2,26},{10... | collective-permute-start | bytes 786440 | tf_op jit(solution)/shard_map/ppermute | solution.py:453
  46.5 0.7 copy-start.9
  68.5 0.8 copy-start.15
  76.8 6.8 %copy-start.29 = (bf16[4,128,512]{2,1,0:T(8,128)(2,1)S(1)}, bf16[4,128,512]{2,1,0:T(8,128)(2,1)}, u32[]{:S(2)}) copy-start(bf16[4,128,512]{2,1,0:T(8,128)(2,1)} %get-tuple-element.39) | copy-start | bytes 1572868
  82.8 2.5 %collective-permute-start.20 = (bf16[4,128,512]{2,1,0:T(8,128)(2,1)}, bf16[4,128,512]{2,1,0:T(8,128)(2,1)S(1)}, u32[]{:S(2)}, u32[]{:S(2)}) collective-permute-start(bf16[4,128,512]{2,1,0:T(8,128)(2,1)} %get-tuple-element.48), channel_id=1, source_target_pairs={{0,1},{1,0},{2,3},{3,2},{4,5},{5,4},{6,7},{7,6},{8,9},{9,8},{10,11... | collective-permute-start | bytes 1572872 | tf_op jit(solution)/shard_map/ppermute | solution.py:453
  83.6 25.6 %collective-permute-start.10 = (bf16[4,128,512]{2,1,0:T(8,128)(2,1)S(1)}, bf16[4,128,512]{2,1,0:T(8,128)(2,1)S(1)}, u32[]{:S(2)}, u32[]{:S(2)}) collective-permute-start(bf16[4,128,512]{2,1,0:T(8,128)(2,1)S(1)} %copy-done.29), channel_id=1, source_target_pairs={{0,1},{1,0},{2,3},{3,2},{4,5},{5,4},{6,7},{7,6},{8,9},{9,8},{10,11... | collective-permute-start | bytes 1572872 | tf_op jit(solution)/shard_map/ppermute | solution.py:453
  85.3 0.8 copy-start.1
  88.2 24.4 %collective-permute-start.21 = (bf16[128,512]{1,0:T(8,128)(2,1)}, bf16[128,512]{1,0:T(8,128)(2,1)S(1)}, u32[]{:S(2)}, u32[]{:S(2)}) collective-permute-start(bf16[128,512]{1,0:T(8,128)(2,1)} %get-tuple-element.50), channel_id=1, source_target_pairs={{0,2},{1,3},{2,0},{3,1},{4,6},{5,7},{6,4},{7,5},{8,10},{9,11},{10,... | collective-permute-start | bytes 393224 | tf_op jit(solution)/shard_map/ppermute | solution.py:453
  88.2 27.4 %collective-permute-start.22 = (bf16[128,512]{1,0:T(8,128)(2,1)}, bf16[128,512]{1,0:T(8,128)(2,1)S(1)}, u32[]{:S(2)}, u32[]{:S(2)}) collective-permute-start(bf16[128,512]{1,0:T(8,128)(2,1)} %get-tuple-element.51), channel_id=1, source_target_pairs={{0,4},{1,5},{2,6},{3,7},{4,0},{5,1},{6,2},{7,3},{8,12},{9,13},{10,... | collective-permute-start | bytes 393224 | tf_op jit(solution)/shard_map/ppermute | solution.py:453
  88.4 27.2 %collective-permute-start.23 = (bf16[128,512]{1,0:T(8,128)(2,1)}, bf16[128,512]{1,0:T(8,128)(2,1)S(1)}, u32[]{:S(2)}, u32[]{:S(2)}) collective-permute-start(bf16[128,512]{1,0:T(8,128)(2,1)} %get-tuple-element.52), channel_id=1, source_target_pairs={{0,6},{1,7},{2,4},{3,5},{4,2},{5,3},{6,0},{7,1},{8,14},{9,15},{10,... | collective-permute-start | bytes 393224 | tf_op jit(solution)/shard_map/ppermute | solution.py:453
  109.2 0.8 copy-start
  112.1 14.6 %collective-permute-start.11 = (bf16[128,512]{1,0:T(8,128)(2,1)}, bf16[128,512]{1,0:T(8,128)(2,1)S(1)}, u32[]{:S(2)}, u32[]{:S(2)}) collective-permute-start(bf16[128,512]{1,0:T(8,128)(2,1)} %get-tuple-element.41), channel_id=1, source_target_pairs={{0,2},{1,3},{2,0},{3,1},{4,6},{5,7},{6,4},{7,5},{8,10},{9,11},{10,... | collective-permute-start | bytes 393224 | tf_op jit(solution)/shard_map/ppermute | solution.py:453
  112.1 16.1 %collective-permute-start.12 = (bf16[128,512]{1,0:T(8,128)(2,1)}, bf16[128,512]{1,0:T(8,128)(2,1)S(1)}, u32[]{:S(2)}, u32[]{:S(2)}) collective-permute-start(bf16[128,512]{1,0:T(8,128)(2,1)} %get-tuple-element.42), channel_id=1, source_target_pairs={{0,4},{1,5},{2,6},{3,7},{4,0},{5,1},{6,2},{7,3},{8,12},{9,13},{10,... | collective-permute-start | bytes 393224 | tf_op jit(solution)/shard_map/ppermute | solution.py:453
  112.6 3.0 %copy-start.25 = (bf16[128,512]{1,0:T(8,128)(2,1)}, bf16[128,512]{1,0:T(8,128)(2,1)S(1)}, u32[]{:S(2)}) copy-start(bf16[128,512]{1,0:T(8,128)(2,1)S(1)} %collective-permute-done.21.refs_1_) | copy-start | bytes 393220
  112.6 15.6 %collective-permute-start.13 = (bf16[128,512]{1,0:T(8,128)(2,1)}, bf16[128,512]{1,0:T(8,128)(2,1)S(1)}, u32[]{:S(2)}, u32[]{:S(2)}) collective-permute-start(bf16[128,512]{1,0:T(8,128)(2,1)} %get-tuple-element.43), channel_id=1, source_target_pairs={{0,6},{1,7},{2,4},{3,5},{4,2},{5,3},{6,0},{7,1},{8,14},{9,15},{10,... | collective-permute-start | bytes 393224 | tf_op jit(solution)/shard_map/ppermute | solution.py:453
  123.8 15.5 %collective-permute-start.24 = (bf16[128,1024]{1,0:T(8,128)(2,1)S(1)}, bf16[128,1024]{1,0:T(8,128)(2,1)S(1)}, u32[]{:S(2)}, u32[]{:S(2)}) collective-permute-start(bf16[128,1024]{1,0:T(8,128)(2,1)S(1)} %get-tuple-element.55), channel_id=1, source_target_pairs={{0,8},{8,0},{16,24},{24,16},{1,9},{9,1},{17,25},{25,17},{2,10},{10... | collective-permute-start | bytes 786440 | tf_op jit(solution)/shard_map/ppermute | solution.py:453
  123.9 21.4 %collective-permute-start.25 = (bf16[128,1024]{1,0:T(8,128)(2,1)S(1)}, bf16[128,1024]{1,0:T(8,128)(2,1)S(1)}, u32[]{:S(2)}, u32[]{:S(2)}) collective-permute-start(bf16[128,1024]{1,0:T(8,128)(2,1)S(1)} %get-tuple-element.54), channel_id=1, source_target_pairs={{0,16},{8,24},{16,0},{24,8},{1,17},{9,25},{17,1},{25,9},{2,18},{10... | collective-permute-start | bytes 786440 | tf_op jit(solution)/shard_map/ppermute | solution.py:453
  126.6 1.6 copy-start.23
  126.6 18.7 %collective-permute-start.26 = (bf16[128,1024]{1,0:T(8,128)(2,1)S(1)}, bf16[128,1024]{1,0:T(8,128)(2,1)S(1)}, u32[]{:S(2)}, u32[]{:S(2)}) collective-permute-start(bf16[128,1024]{1,0:T(8,128)(2,1)S(1)} %get-tuple-element.53), channel_id=1, source_target_pairs={{0,24},{8,16},{16,8},{24,0},{1,25},{9,17},{17,9},{25,1},{2,26},{10... | collective-permute-start | bytes 786440 | tf_op jit(solution)/shard_map/ppermute | solution.py:453
  136.4 12.7 %collective-permute-start.14 = (bf16[128,1024]{1,0:T(8,128)(2,1)S(1)}, bf16[128,1024]{1,0:T(8,128)(2,1)S(1)}, u32[]{:S(2)}, u32[]{:S(2)}) collective-permute-start(bf16[128,1024]{1,0:T(8,128)(2,1)S(1)} %get-tuple-element.59), channel_id=1, source_target_pairs={{0,8},{8,0},{16,24},{24,16},{1,9},{9,1},{17,25},{25,17},{2,10},{10... | collective-permute-start | bytes 786440 | tf_op jit(solution)/shard_map/ppermute | solution.py:453
  136.4 31.3 %collective-permute-start.15 = (bf16[128,1024]{1,0:T(8,128)(2,1)S(1)}, bf16[128,1024]{1,0:T(8,128)(2,1)S(1)}, u32[]{:S(2)}, u32[]{:S(2)}) collective-permute-start(bf16[128,1024]{1,0:T(8,128)(2,1)S(1)} %get-tuple-element.58), channel_id=1, source_target_pairs={{0,16},{8,24},{16,0},{24,8},{1,17},{9,25},{17,1},{25,9},{2,18},{10... | collective-permute-start | bytes 786440 | tf_op jit(solution)/shard_map/ppermute | solution.py:453
  139.3 28.5 %copy-start.17 = (bf16[128,1024]{1,0:T(8,128)(2,1)}, bf16[128,1024]{1,0:T(8,128)(2,1)S(1)}, u32[]{:S(2)}) copy-start(bf16[128,1024]{1,0:T(8,128)(2,1)S(1)} %collective-permute-done.24.refs_5_) | copy-start | bytes 786436
  139.3 28.5 %collective-permute-start.16 = (bf16[128,1024]{1,0:T(8,128)(2,1)S(1)}, bf16[128,1024]{1,0:T(8,128)(2,1)S(1)}, u32[]{:S(2)}, u32[]{:S(2)}) collective-permute-start(bf16[128,1024]{1,0:T(8,128)(2,1)S(1)} %get-tuple-element.57), channel_id=1, source_target_pairs={{0,24},{8,16},{16,8},{24,0},{1,25},{9,17},{17,9},{25,1},{2,26},{10... | collective-permute-start | bytes 786440 | tf_op jit(solution)/shard_map/ppermute | solution.py:453
  145.3 22.5 %copy-start.18 = (bf16[128,1024]{1,0:T(8,128)(2,1)}, bf16[128,1024]{1,0:T(8,128)(2,1)S(1)}, u32[]{:S(2)}) copy-start(bf16[128,1024]{1,0:T(8,128)(2,1)S(1)} %collective-permute-done.25.refs_6_) | copy-start | bytes 786436
  145.3 22.5 %copy-start.19 = (bf16[128,1024]{1,0:T(8,128)(2,1)}, bf16[128,1024]{1,0:T(8,128)(2,1)S(1)}, u32[]{:S(2)}) copy-start(bf16[128,1024]{1,0:T(8,128)(2,1)S(1)} %collective-permute-done.26.refs_7_) | copy-start | bytes 786436
  149.1 18.7 %copy-start.20 = (bf16[128,1024]{1,0:T(8,128)(2,1)}, bf16[128,1024]{1,0:T(8,128)(2,1)S(1)}, u32[]{:S(2)}) copy-start(bf16[128,1024]{1,0:T(8,128)(2,1)S(1)} %collective-permute-done.14.refs_1_) | copy-start | bytes 786436
  167.8 0.8 copy-start.22
  (9 other events, 6.3 us)

commit v3 on v2

--- a/solution.py
+++ b/solution.py
@@ -30,7 +30,7 @@
 
 
 def params():
-    return pltpu.CompilerParams(vmem_limit_bytes=56 * MIB)
+    return pltpu.CompilerParams(vmem_limit_bytes=20 * MIB)
 
 
 def cost(flops, moved):
@@ -157,28 +157,28 @@
 
 
 def query_terms_body(me, dq_ref, w_ref, out_ref):
-    out_ref[0] = mm_nt(dq_ref[...], w_ref[...])
-
-
-def query_terms(dq, w, size):
+    out_ref[...] = mm_nt(dq_ref[...], w_ref[...])
+
+
+def query_terms(dq, w, size, k):
     rows, depth = dq.shape
     share = w.shape[0] // size
-    part = min(share, 512)
+    part = min(share, 256)
     count = share // part
     return pl.pallas_call(
         query_terms_body,
         grid_spec=pltpu.PrefetchScalarGridSpec(
             num_scalar_prefetch=1,
-            grid=(size, count),
+            grid=(count,),
             in_specs=[
-                pl.BlockSpec((rows, depth), lambda k, i, me: (0, 0)),
-                pl.BlockSpec((part, depth), lambda k, i, me: ((me[0] ^ k) * count + i, 0)),
+                pl.BlockSpec((rows, depth), lambda i, me: (0, 0)),
+                pl.BlockSpec((part, depth), lambda i, me: ((me[0] ^ k) * count + i, 0)),
             ],
-            out_specs=pl.BlockSpec((1, rows, part), lambda k, i, me: (k, 0, i)),
+            out_specs=pl.BlockSpec((rows, part), lambda i, me: (0, i)),
         ),
-        out_shape=jax.ShapeDtypeStruct((size, rows, share), jnp.float32),
-        compiler_params=params(),
-        cost_estimate=cost(2 * rows * w.size, 2 * w.size + 4 * rows * w.shape[0]),
+        out_shape=jax.ShapeDtypeStruct((rows, share), jnp.float32),
+        compiler_params=params(),
+        cost_estimate=cost(2 * rows * share * depth, 2 * share * depth + 4 * rows * share),
         name="query_terms",
     )(head_index(), dq, w)
 
@@ -188,37 +188,37 @@
     wk_ref, wv_ref, out_ref, grads = refs[count:]
     width = wk_ref.shape[1]
 
-    @pl.when((pl.program_id(0) == 0) & (pl.program_id(1) == 0))
+    @pl.when(pl.program_id(0) == 0)
     def _():
         total = terms[0][...].astype(jnp.float32)
         for term in terms[1:]:
             total = total + term[...].astype(jnp.float32)
         grads[...] = total.astype(grads.dtype)
 
-    total = first_ref[0] + mm_nt(grads[:, :width], wk_ref[...])
+    total = first_ref[...] + mm_nt(grads[:, :width], wk_ref[...])
     total = total + mm_nt(grads[:, width:], wv_ref[...])
-    out_ref[0] = total.astype(out_ref.dtype)
-
-
-def all_terms(first, terms, wk, wv):
-    size, rows, share = first.shape
+    out_ref[...] = total.astype(out_ref.dtype)
+
+
+def all_terms(first, terms, wk, wv, k):
+    rows, share = first.shape
     width = wk.shape[1]
-    part = min(share, 1024)
+    part = min(share, 512)
     count = share // part
     return pl.pallas_call(
         functools.partial(all_terms_body, len(terms)),
         grid_spec=pltpu.PrefetchScalarGridSpec(
             num_scalar_prefetch=1,
-            grid=(size, count),
-            in_specs=[pl.BlockSpec((1, rows, part), lambda k, i, me: (k, 0, i))]
-            + [pl.BlockSpec((rows, 2 * width), lambda k, i, me: (0, 0))] * len(terms)
-            + [pl.BlockSpec((part, width), lambda k, i, me: ((me[0] ^ k) * count + i, 0))] * 2,
-            out_specs=pl.BlockSpec((1, rows, part), lambda k, i, me: (k, 0, i)),
+            grid=(count,),
+            in_specs=[pl.BlockSpec((rows, part), lambda i, me: (0, i))]
+            + [pl.BlockSpec((rows, 2 * width), lambda i, me: (0, 0))] * len(terms)
+            + [pl.BlockSpec((part, width), lambda i, me: ((me[0] ^ k) * count + i, 0))] * 2,
+            out_specs=pl.BlockSpec((rows, part), lambda i, me: (0, i)),
             scratch_shapes=[VMEM((rows, 2 * width), jnp.bfloat16)],
         ),
-        out_shape=jax.ShapeDtypeStruct((size, rows, share), jnp.bfloat16),
-        compiler_params=params(),
-        cost_estimate=cost(4 * rows * wk.size, 4 * wk.size + 6 * first.size),
+        out_shape=jax.ShapeDtypeStruct((rows, share), jnp.bfloat16),
+        compiler_params=params(),
+        cost_estimate=cost(4 * rows * share * width, 4 * share * width + 6 * rows * share),
         name="all_terms",
     )(head_index(), first, *terms, wk, wv)
 
@@ -463,10 +463,6 @@
     return [x] + [swap(x, k, "head") for k in range(1, lax.axis_size("head"))]
 
 
-def scatter_head(x):
-    return [x[0]] + [swap(x[k], k, "head") for k in range(1, lax.axis_size("head"))]
-
-
 def pair_body(even_ref, odd_ref, *outs):
     for k, out in enumerate(outs):
         out[...] = (
@@ -501,6 +497,16 @@
         doc_lengths.shape[0],
     )
     heads = lax.axis_size("head")
+
+    def scatter_head(query_grad, even, odd):
+        first = [query_terms(query_grad, w_query, heads, k) for k in range(heads)]
+        terms = scatter_ctx(even, odd)
+        got = []
+        for k in list(range(1, heads)) + [0]:
+            part = all_terms(first[k], terms, w_key, value_projection, k)
+            got.append(swap(part, k, "head") if k else part)
+        return got, part
+
     upper_out, lower_out = split_rows(out_grad, span_order)
     upper_out = gather_head(upper_out)
     own = project_kv(inputs, w_key, value_projection)
@@ -513,16 +519,14 @@
     query_grad, even, odd, rest = grads(
         True, query, context_grad, level, mixed, (), blocks, span_order, doc_lengths, sizes
     )
-    first = query_terms(query_grad, w_query, heads)
-    terms = scatter_ctx(even, odd)
-    upper = scatter_head(all_terms(first, terms, w_key, value_projection))
+    upper, last = scatter_head(query_grad, even, odd)
+    lower_out, last = lax.optimization_barrier((lower_out, last))
+    upper[-1] = last
     context_grad = back_project(lower_out, w_out)
     query_grad, even, odd = grads(
         False, query, context_grad, level, mixed, (rest,), blocks, span_order, doc_lengths, sizes
     )
-    first = query_terms(query_grad, w_query, heads)
-    terms = scatter_ctx(even, odd)
-    lower = scatter_head(all_terms(first, terms, w_key, value_projection))
+    lower, last = scatter_head(query_grad, even, odd)
     return join_rows(upper, lower, span_order)
 
 

time: 173 us -> 150 us (0.87); the launches traced: 171 us -> 150 us
  Pallas kernels: 89.9 us -> 46.4 us
  starting transfers between devices: 33.1 us -> 43.9 us
  local copies, waits for them, and re-layouts: 10.8 us -> 16.9 us
  waiting for transfers between devices: 37.1 us -> 42.4 us
    ppermute x27, starting transfers between devices: 33.1 us -> 43.9 us  [swap(): lax.ppermute(x, axis, [(i, i ^ k) for i in range(lax.axis_size(axis))])]
    unnamed x60 -> x66, local copies, waits for them, and re-layouts: 6.88 us -> 16.9 us
    pallas_call x2, Pallas kernels: 16.9 us -> 6.92 us  [grads(): pl.pallas_call(functools.partial(grads_body, sizes, upper), in_specs=[pl....]
    pallas_call x2 -> x8, Pallas kernels: 17.5 us -> 10.5 us  [query_terms(): pl.pallas_call(query_terms_body, grid_spec=pltpu.PrefetchScalarGridSpec(n...]
    pallas_call x1, Pallas kernels: 10.4 us -> 4.7 us  [stats(): pl.pallas_call(functools.partial(stats_body, sizes), in_specs=[pl.BlockSp...]
    ppermute x27, waiting for transfers between devices: 37.1 us -> 42.4 us  [swap(): lax.ppermute(x, axis, [(i, i ^ k) for i in range(lax.axis_size(axis))])]
    pallas_call x2, Pallas kernels: 13.5 us -> 8.12 us  [back_project(): pl.pallas_call(back_body, grid=(width // part,), in_specs=[pl.BlockSpec((...]
    pallas_call x2 -> x8, Pallas kernels: 11.2 us -> 6.33 us  [all_terms(): pl.pallas_call(functools.partial(all_terms_body, len(terms)), grid_spec=p...]
  transfers between devices with their start and end apart: 27 -> 27, of which waited for: 7 -> 8; matrix products, arithmetic and copies ran while one was open for 2% -> 0% of each run, Pallas kernels for 42% -> 18%
where the time goes in v3:
time: 150 us
  Pallas kernels  46.4 us (31%)
  starting transfers between devices  43.9 us (29%)
  waiting for transfers between devices  42.4 us (28%)
  local copies, waits for them, and re-layouts  16.9 us (11%)
    ppermute x27, starting transfers between devices, swap(): lax.ppermute(x, axis, [(i, i ^ k) for i in range(lax.axis_size(axis))])  43.9 us
    ppermute x27, waiting for transfers between devices, swap(): lax.ppermute(x, axis, [(i, i ^ k) for i in range(lax.axis_size(axis))])  42.4 us
    unnamed x66, local copies, waits for them, and re-layouts  16.9 us
    pallas_call x8, Pallas kernels, query_terms(): pl.pallas_call(query_terms_body, grid_spec=pltpu.PrefetchScalarGridSpec(n...  10.5 us
    pallas_call x2, Pallas kernels, back_project(): pl.pallas_call(back_body, grid=(width // part,), in_specs=[pl.BlockSpec((...  8.12 us
    pallas_call x2, Pallas kernels, grads(): pl.pallas_call(functools.partial(grads_body, sizes, upper), in_specs=[pl....  6.92 us
    pallas_call x8, Pallas kernels, all_terms(): pl.pallas_call(functools.partial(all_terms_body, len(terms)), grid_spec=p...  6.33 us
    pallas_call x1, Pallas kernels, stats(): pl.pallas_call(functools.partial(stats_body, sizes), in_specs=[pl.BlockSp...  4.7 us
  transfers between devices with their start and end apart: 27, of which 8 were waited for; matrix products, arithmetic and copies ran while one was open for 0% of the time, Pallas kernels for 18%

profile of v3, /device:TPU:0, one launch (start us, length us, event | category | flops | bytes accessed | tf_op | source)
XLA Modules:
  0.0 150.3 jit_solution(11140185113360086988)
XLA Ops:
  0.0 1.0 copy-done.13
  1.7 1.3 split_rows.1
  3.0 3.0 %collective-permute-start = (bf16[128,1024]{1,0:T(8,128)(2,1)S(1)}, bf16[128,1024]{1,0:T(8,128)(2,1)S(1)}, u32[]{:S(2)}, u32[]{:S(2)}) collective-permute-start(bf16[128,1024]{1,0:T(8,128)(2,1)S(1)} %get-tuple-element.36.refs_0_), channel_id=1, source_target_pairs={{0,8},{8,0},{16,24},{24,16},{1,9},{9,1},{17,25},{25,17},{2,10},{10... | collective-permute-start | bytes 786440 | tf_op jit(solution)/shard_map/ppermute | solution.py:453
  6.0 2.6 %collective-permute-start.1 = (bf16[128,1024]{1,0:T(8,128)(2,1)S(1)}, bf16[128,1024]{1,0:T(8,128)(2,1)S(1)}, u32[]{:S(2)}, u32[]{:S(2)}) collective-permute-start(bf16[128,1024]{1,0:T(8,128)(2,1)S(1)} %get-tuple-element.36.refs_0_), channel_id=1, source_target_pairs={{0,16},{8,24},{16,0},{24,8},{1,17},{9,25},{17,1},{25,9},{2,18},{10... | collective-permute-start | bytes 786440 | tf_op jit(solution)/shard_map/ppermute | solution.py:453
  8.6 1.6 %copy-done.2 = bf16[4096,256]{1,0:T(8,128)(2,1)S(1)} copy-done((bf16[4096,256]{1,0:T(8,128)(2,1)S(1)}, bf16[4096,256]{1,0:T(8,128)(2,1)}, u32[]{:S(2)}) %copy-start.2) | copy-done | bytes 2097176
  10.2 1.6 %copy-done.4 = bf16[4096,256]{1,0:T(8,128)(2,1)S(1)} copy-done((bf16[4096,256]{1,0:T(8,128)(2,1)S(1)}, bf16[4096,256]{1,0:T(8,128)(2,1)}, u32[]{:S(2)}) %copy-start.4) | copy-done | bytes 2097176
  11.8 1.6 %copy-done.8 = bf16[256,4096]{1,0:T(8,128)(2,1)S(1)} copy-done((bf16[256,4096]{1,0:T(8,128)(2,1)S(1)}, bf16[256,4096]{1,0:T(8,128)(2,1)}, u32[]{:S(2)}) %copy-start.8) | copy-done | bytes 2097176
  13.4 2.0 %project_kv.1.refs_0_.refs_1_ = bf16[256,512]{1,0:T(8,128)(2,1)S(1)} custom-call(bf16[256,4096]{1,0:T(8,128)(2,1)S(1)} %copy-done.8, bf16[4096,256]{1,0:T(8,128)(2,1)S(1)} %copy-done.2, bf16[4096,256]{1,0:T(8,128)(2,1)S(1)} %copy-done.4), custom_call_target="tpu_custom_call" | custom-call | flops 1073741824 | bytes 6291456 | tf_op jit(solution)/shard_map/project_kv/pallas_call | solution.py:70
  15.4 1.6 %collective-permute-start.4 = (bf16[256,512]{1,0:T(8,128)(2,1)S(1)}, bf16[256,512]{1,0:T(8,128)(2,1)S(1)}, u32[]{:S(2)}, u32[]{:S(2)}) collective-permute-start(bf16[256,512]{1,0:T(8,128)(2,1)S(1)} %project_kv.1.refs_0_.refs_1_), channel_id=1, source_target_pairs={{0,2},{1,3},{2,0},{3,1},{4,6},{5,7},{6,4},{7,5},{8,10},{9,11},{10,... | collective-permute-start | bytes 786440 | tf_op jit(solution)/shard_map/ppermute | solution.py:453
  17.0 1.5 %collective-permute-start.6 = (bf16[256,512]{1,0:T(8,128)(2,1)S(1)}, bf16[256,512]{1,0:T(8,128)(2,1)S(1)}, u32[]{:S(2)}, u32[]{:S(2)}) collective-permute-start(bf16[256,512]{1,0:T(8,128)(2,1)S(1)} %project_kv.1.refs_0_.refs_1_), channel_id=1, source_target_pairs={{0,4},{1,5},{2,6},{3,7},{4,0},{5,1},{6,2},{7,3},{8,12},{9,13},{10,... | collective-permute-start | bytes 786440 | tf_op jit(solution)/shard_map/ppermute | solution.py:453
  19.0 1.5 collective-permute-start.2
  20.5 4.3 %collective-permute-done.4.refs_2_.refs_3_ = bf16[256,512]{1,0:T(8,128)(2,1)S(1)} collective-permute-done((bf16[256,512]{1,0:T(8,128)(2,1)S(1)}, bf16[256,512]{1,0:T(8,128)(2,1)S(1)}, u32[]{:S(2)}, u32[]{:S(2)}) %collective-permute-start.4) | collective-permute-done | bytes 262176 | tf_op jit(solution)/shard_map/ppermute | solution.py:453
  24.7 5.1 %collective-permute-done.6.refs_4_.refs_5_ = bf16[256,512]{1,0:T(8,128)(2,1)S(1)} collective-permute-done((bf16[256,512]{1,0:T(8,128)(2,1)S(1)}, bf16[256,512]{1,0:T(8,128)(2,1)S(1)}, u32[]{:S(2)}, u32[]{:S(2)}) %collective-permute-start.6) | collective-permute-done | bytes 262176 | tf_op jit(solution)/shard_map/ppermute | solution.py:453
  30.3 3.4 %copy-done = bf16[4096,1024]{1,0:T(8,128)(2,1)S(1)} copy-done((bf16[4096,1024]{1,0:T(8,128)(2,1)S(1)}, bf16[4096,1024]{1,0:T(8,128)(2,1)}, u32[]{:S(2)}) %copy-start) | copy-done | bytes 8388632
  33.7 4.1 %project.1.q_ref = bf16[256,1024]{1,0:T(8,128)(2,1)S(1)} custom-call(bf16[256,4096]{1,0:T(8,128)(2,1)S(1)} %copy-done.8, bf16[4096,1024]{1,0:T(8,128)(2,1)S(1)} %copy-done), custom_call_target="tpu_custom_call" | custom-call | flops 2147483648 | bytes 10485760 | tf_op jit(solution)/shard_map/project/pallas_call | solution.py:95
  37.8 3.4 %back_project.2.g_ref = bf16[128,1024]{1,0:T(8,128)(2,1)S(1)} custom-call(bf16[128,1024]{1,0:T(8,128)(2,1)S(1)} %get-tuple-element.36.refs_0_, bf16[128,1024]{1,0:T(8,128)(2,1)S(1)} %collective-permute-done.refs_1_, bf16[128,1024]{1,0:T(8,128)(2,1)S(1)} %collective-permute-done.1.refs_2_, bf16[128,1024]{1,0:T(8,128)(2,1)S(1)} %collective-permute-done.2.refs_3_, ...), custom_call_target="tpu_custom_call" | custom-call | flops 1073741824 | bytes 8388608 | tf_op jit(solution)/shard_map/back_project/pallas_call | solution.py:146
  41.3 4.7 %stats.1 = (f32[4,1,512]{2,1,0:T(1,128)S(1)}, f32[4,128,512]{2,1,0:T(8,128)S(1)}) custom-call(s32[16]{0:T(128)S(1)} %copy-done.29, s32[8]{0:T(128)S(1)} %copy-done.30, bf16[256,1024]{1,0:T(8,128)(2,1)S(1)} %project.1.q_ref, bf16[256,512]{1,0:T(8,128)(2,1)S(1)} %project_kv.1.refs_0_.refs_1_, bf16[256,512]{1,0:T(8,128)(2,1)S(1)} %collective-permute-done.3.refs_1_.refs_2_, ...), custom_call_target="tpu_custom_call" | custom-call | flops 1207959552 | bytes 6291456 | tf_op jit(solution)/shard_map/stats/pallas_call | solution.py:335
  46.1 3.9 %upper_grads.1 = (bf16[128,1024]{1,0:T(8,128)(2,1)S(1)}, bf16[4,128,512]{2,1,0:T(8,128)(2,1)S(1)}, bf16[4,128,512]{2,1,0:T(8,128)(2,1)S(1)}, f32[1024,512]{1,0:T(8,128)S(1)}) custom-call(s32[16]{0:T(128)S(1)} %copy-done.29, s32[8]{0:T(128)S(1)} %copy-done.30, bf16[256,1024]{1,0:T(8,128)(2,1)S(1)} %project.1.q_ref, bf16[128,1024]{1,0:T(8,128)(2,1)S(1)} %back_project.2.g_ref, ...), custom_call_target="tpu_custom_call" | custom-call | flops 1610612736 | bytes 8388608 | tf_op jit(solution)/shard_map/upper_grads/pallas_call | solution.py:435
  50.1 1.9 %collective-permute-done.10.odd_ref = bf16[4,128,512]{2,1,0:T(8,128)(2,1)S(1)} collective-permute-done((bf16[4,128,512]{2,1,0:T(8,128)(2,1)S(1)}, bf16[4,128,512]{2,1,0:T(8,128)(2,1)S(1)}, u32[]{:S(2)}, u32[]{:S(2)}) %collective-permute-start.10) | collective-permute-done | bytes 524320 | tf_op jit(solution)/shard_map/ppermute | solution.py:453
  52.7 10.4 %collective-permute-start.11 = (bf16[128,512]{1,0:T(8,128)(2,1)S(1)}, bf16[128,512]{1,0:T(8,128)(2,1)S(1)}, u32[]{:S(2)}, u32[]{:S(2)}) collective-permute-start(bf16[128,512]{1,0:T(8,128)(2,1)S(1)} %get-tuple-element.46), channel_id=1, source_target_pairs={{0,2},{1,3},{2,0},{3,1},{4,6},{5,7},{6,4},{7,5},{8,10},{9,11},{10,... | collective-permute-start | bytes 393224 | tf_op jit(solution)/shard_map/ppermute | solution.py:453
  63.6 1.1 collective-permute-start.18
  64.7 2.8 %collective-permute-start.19 = (bf16[128,1024]{1,0:T(8,128)(2,1)}, bf16[128,1024]{1,0:T(8,128)(2,1)}, u32[]{:S(2)}, u32[]{:S(2)}) collective-permute-start(bf16[128,1024]{1,0:T(8,128)(2,1)} %get-tuple-element.51.refs_0_), channel_id=1, source_target_pairs={{0,24},{8,16},{16,8},{24,0},{1,25},{9,17},{17,9},{25,1},{2,26},{10... | collective-permute-start | bytes 786440 | tf_op jit(solution)/shard_map/ppermute | solution.py:453
  67.5 2.0 %collective-permute-start.12 = (bf16[128,512]{1,0:T(8,128)(2,1)}, bf16[128,512]{1,0:T(8,128)(2,1)S(1)}, u32[]{:S(2)}, u32[]{:S(2)}) collective-permute-start(bf16[128,512]{1,0:T(8,128)(2,1)} %get-tuple-element.47), channel_id=1, source_target_pairs={{0,4},{1,5},{2,6},{3,7},{4,0},{5,1},{6,2},{7,3},{8,12},{9,13},{10,... | collective-permute-start | bytes 393224 | tf_op jit(solution)/shard_map/ppermute | solution.py:453
  70.1 3.4 %copy-done.1 = bf16[4096,1024]{1,0:T(8,128)(2,1)S(1)} copy-done((bf16[4096,1024]{1,0:T(8,128)(2,1)S(1)}, bf16[4096,1024]{1,0:T(8,128)(2,1)}, u32[]{:S(2)}) %copy-start.1) | copy-done | bytes 8388632
  73.5 1.3 query_terms.11.first_ref
  76.5 8.7 %collective-permute-done.18.refs_2_ = bf16[128,1024]{1,0:T(8,128)(2,1)} collective-permute-done((bf16[128,1024]{1,0:T(8,128)(2,1)}, bf16[128,1024]{1,0:T(8,128)(2,1)}, u32[]{:S(2)}, u32[]{:S(2)}) %collective-permute-start.18) | collective-permute-done | bytes 262176 | tf_op jit(solution)/shard_map/ppermute | solution.py:453
  85.3 3.4 %copy-done.7 = bf16[1024,4096]{1,0:T(8,128)(2,1)S(1)} copy-done((bf16[1024,4096]{1,0:T(8,128)(2,1)S(1)}, bf16[1024,4096]{1,0:T(8,128)(2,1)}, u32[]{:S(2)}) %copy-start.7) | copy-done | bytes 8388632
  88.7 4.7 %back_project.3.g_ref = bf16[128,1024]{1,0:T(8,128)(2,1)S(1)} custom-call(bf16[128,1024]{1,0:T(8,128)(2,1)} %get-tuple-element.51.refs_0_, bf16[128,1024]{1,0:T(8,128)(2,1)} %collective-permute-done.17.refs_1_, bf16[128,1024]{1,0:T(8,128)(2,1)} %collective-permute-done.18.refs_2_, bf16[128,1024]{1,0:T(8,128)(2,1)} %collective-permute-done.19.refs_3_, ...), custom_call_target="tpu_custom_call" | custom-call | flops 1073741824 | bytes 8388608 | tf_op jit(solution)/shard_map/back_project/pallas_call | solution.py:146
  93.5 3.0 %lower_grads.1 = (bf16[128,1024]{1,0:T(8,128)(2,1)S(1)}, bf16[4,128,512]{2,1,0:T(8,128)(2,1)S(1)}, bf16[4,128,512]{2,1,0:T(8,128)(2,1)S(1)}) custom-call(s32[16]{0:T(128)S(1)} %copy-done.29, s32[8]{0:T(128)S(1)} %copy-done.30, bf16[256,1024]{1,0:T(8,128)(2,1)S(1)} %project.1.q_ref, bf16[128,1024]{1,0:T(8,128)(2,1)S(1)} %back_project.3.g_ref, ...), custom_call_target="tpu_custom_call" | custom-call | flops 805306368 | bytes 8388608 | tf_op jit(solution)/shard_map/lower_grads/pallas_call | solution.py:435
  96.7 1.3 query_terms.10.first_ref
  98.8 1.4 collective-permute-start.16
  100.4 2.3 %collective-permute-start.21 = (bf16[128,512]{1,0:T(8,128)(2,1)S(1)}, bf16[128,512]{1,0:T(8,128)(2,1)S(1)}, u32[]{:S(2)}, u32[]{:S(2)}) collective-permute-start(bf16[128,512]{1,0:T(8,128)(2,1)S(1)} %get-tuple-element.60), channel_id=1, source_target_pairs={{0,2},{1,3},{2,0},{3,1},{4,6},{5,7},{6,4},{7,5},{8,10},{9,11},{10,... | collective-permute-start | bytes 393224 | tf_op jit(solution)/shard_map/ppermute | solution.py:453
  102.7 1.2 collective-permute-start.22
  104.2 1.3 query_terms.9.first_ref
  105.5 1.3 query_terms.8.first_ref
  107.7 5.3 %collective-permute-start.15 = (bf16[128,1024]{1,0:T(8,128)(2,1)S(1)}, bf16[128,1024]{1,0:T(8,128)(2,1)S(1)}, u32[]{:S(2)}, u32[]{:S(2)}) collective-permute-start(bf16[128,1024]{1,0:T(8,128)(2,1)S(1)} %all_terms.9), channel_id=1, source_target_pairs={{0,16},{8,24},{16,0},{24,8},{1,17},{9,25},{17,1},{25,9},{2,18},{10... | collective-permute-start | bytes 786440 | tf_op jit(solution)/shard_map/ppermute | solution.py:453
  113.7 1.3 query_terms.14.first_ref
  115.1 1.3 query_terms.13.first_ref
  116.4 1.3 query_terms.12.first_ref
  117.9 0.8 all_terms.14
  118.7 1.5 %collective-permute-start.26 = (bf16[128,1024]{1,0:T(8,128)(2,1)S(1)}, bf16[128,1024]{1,0:T(8,128)(2,1)S(1)}, u32[]{:S(2)}, u32[]{:S(2)}) collective-permute-start(bf16[128,1024]{1,0:T(8,128)(2,1)S(1)} %all_terms.14), channel_id=1, source_target_pairs={{0,24},{8,16},{16,8},{24,0},{1,25},{9,17},{17,9},{25,1},{2,26},{10... | collective-permute-start | bytes 786440 | tf_op jit(solution)/shard_map/ppermute | solution.py:453
  121.0 2.1 %collective-permute-start.25 = (bf16[128,1024]{1,0:T(8,128)(2,1)S(1)}, bf16[128,1024]{1,0:T(8,128)(2,1)S(1)}, u32[]{:S(2)}, u32[]{:S(2)}) collective-permute-start(bf16[128,1024]{1,0:T(8,128)(2,1)S(1)} %all_terms.13), channel_id=1, source_target_pairs={{0,16},{8,24},{16,0},{24,8},{1,17},{9,25},{17,1},{25,9},{2,18},{10... | collective-permute-start | bytes 786440 | tf_op jit(solution)/shard_map/ppermute | solution.py:453
  123.8 1.0 collective-permute-start.24
  124.8 1.3 query_terms.15.first_ref
  126.1 0.8 all_terms.15.refs_7_
  127.0 10.2 %collective-permute-done.15.refs_1_ = bf16[128,1024]{1,0:T(8,128)(2,1)S(1)} collective-permute-done((bf16[128,1024]{1,0:T(8,128)(2,1)S(1)}, bf16[128,1024]{1,0:T(8,128)(2,1)S(1)}, u32[]{:S(2)}, u32[]{:S(2)}) %collective-permute-start.15) | collective-permute-done | bytes 262176 | tf_op jit(solution)/shard_map/ppermute | solution.py:453
  137.6 11.1 %collective-permute-done.25.refs_5_ = bf16[128,1024]{1,0:T(8,128)(2,1)S(1)} collective-permute-done((bf16[128,1024]{1,0:T(8,128)(2,1)S(1)}, bf16[128,1024]{1,0:T(8,128)(2,1)S(1)}, u32[]{:S(2)}, u32[]{:S(2)}) %collective-permute-start.25) | collective-permute-done | bytes 262176 | tf_op jit(solution)/shard_map/ppermute | solution.py:453
  148.7 1.6 %join_rows.1 = bf16[256,1024]{1,0:T(8,128)(2,1)} custom-call(s32[16]{0:T(128)S(1)} %copy-done.29, bf16[128,1024]{1,0:T(8,128)(2,1)S(1)} %collective-permute-done.14.refs_0_, bf16[128,1024]{1,0:T(8,128)(2,1)S(1)} %collective-permute-done.15.refs_1_, bf16[128,1024]{1,0:T(8,128)(2,1)S(1)} %collective-permute-done.16.refs_2_, ...), custom_call_target="tpu_custom_call" | custom-call | flops 1048576 | bytes 2621440 | tf_op jit(solution)/shard_map/join_rows/pallas_call | solution.py:239
  (100 shorter events, 10.2 us)
Async XLA Ops:
  3.0 16.0 %collective-permute-start = (bf16[128,1024]{1,0:T(8,128)(2,1)S(1)}, bf16[128,1024]{1,0:T(8,128)(2,1)S(1)}, u32[]{:S(2)}, u32[]{:S(2)}) collective-permute-start(bf16[128,1024]{1,0:T(8,128)(2,1)S(1)} %get-tuple-element.36.refs_0_), channel_id=1, source_target_pairs={{0,8},{8,0},{16,24},{24,16},{1,9},{9,1},{17,25},{25,17},{2,10},{10... | collective-permute-start | bytes 786440 | tf_op jit(solution)/shard_map/ppermute | solution.py:453
  6.0 14.5 %collective-permute-start.1 = (bf16[128,1024]{1,0:T(8,128)(2,1)S(1)}, bf16[128,1024]{1,0:T(8,128)(2,1)S(1)}, u32[]{:S(2)}, u32[]{:S(2)}) collective-permute-start(bf16[128,1024]{1,0:T(8,128)(2,1)S(1)} %get-tuple-element.36.refs_0_), channel_id=1, source_target_pairs={{0,16},{8,24},{16,0},{24,8},{1,17},{9,25},{17,1},{25,9},{2,18},{10... | collective-permute-start | bytes 786440 | tf_op jit(solution)/shard_map/ppermute | solution.py:453
  15.4 30.6 %copy-start.11 = (bf16[256,512]{1,0:T(8,128)(2,1)}, bf16[256,512]{1,0:T(8,128)(2,1)S(1)}, u32[]{:S(2)}) copy-start(bf16[256,512]{1,0:T(8,128)(2,1)S(1)} %project_kv.1.refs_0_.refs_1_) | copy-start | bytes 786436
  15.4 9.3 %collective-permute-start.4 = (bf16[256,512]{1,0:T(8,128)(2,1)S(1)}, bf16[256,512]{1,0:T(8,128)(2,1)S(1)}, u32[]{:S(2)}, u32[]{:S(2)}) collective-permute-start(bf16[256,512]{1,0:T(8,128)(2,1)S(1)} %project_kv.1.refs_0_.refs_1_), channel_id=1, source_target_pairs={{0,2},{1,3},{2,0},{3,1},{4,6},{5,7},{6,4},{7,5},{8,10},{9,11},{10,... | collective-permute-start | bytes 786440 | tf_op jit(solution)/shard_map/ppermute | solution.py:453
  17.0 12.8 %collective-permute-start.6 = (bf16[256,512]{1,0:T(8,128)(2,1)S(1)}, bf16[256,512]{1,0:T(8,128)(2,1)S(1)}, u32[]{:S(2)}, u32[]{:S(2)}) collective-permute-start(bf16[256,512]{1,0:T(8,128)(2,1)S(1)} %project_kv.1.refs_0_.refs_1_), channel_id=1, source_target_pairs={{0,4},{1,5},{2,6},{3,7},{4,0},{5,1},{6,2},{7,3},{8,12},{9,13},{10,... | collective-permute-start | bytes 786440 | tf_op jit(solution)/shard_map/ppermute | solution.py:453
  18.5 11.3 %collective-permute-start.8 = (bf16[256,512]{1,0:T(8,128)(2,1)S(1)}, bf16[256,512]{1,0:T(8,128)(2,1)S(1)}, u32[]{:S(2)}, u32[]{:S(2)}) collective-permute-start(bf16[256,512]{1,0:T(8,128)(2,1)S(1)} %project_kv.1.refs_0_.refs_1_), channel_id=1, source_target_pairs={{0,6},{1,7},{2,4},{3,5},{4,2},{5,3},{6,0},{7,1},{8,14},{9,15},{10,... | collective-permute-start | bytes 786440 | tf_op jit(solution)/shard_map/ppermute | solution.py:453
  19.0 18.8 %collective-permute-start.2 = (bf16[128,1024]{1,0:T(8,128)(2,1)S(1)}, bf16[128,1024]{1,0:T(8,128)(2,1)S(1)}, u32[]{:S(2)}, u32[]{:S(2)}) collective-permute-start(bf16[128,1024]{1,0:T(8,128)(2,1)S(1)} %get-tuple-element.36.refs_0_), channel_id=1, source_target_pairs={{0,24},{8,16},{16,8},{24,0},{1,25},{9,17},{17,9},{25,1},{2,26},{10... | collective-permute-start | bytes 786440 | tf_op jit(solution)/shard_map/ppermute | solution.py:453
  20.5 20.8 %collective-permute-start.3 = (bf16[256,512]{1,0:T(8,128)(2,1)S(1)}, bf16[256,512]{1,0:T(8,128)(2,1)S(1)}, u32[]{:S(2)}, u32[]{:S(2)}) collective-permute-start(bf16[256,512]{1,0:T(8,128)(2,1)S(1)} %project_kv.1.refs_0_.refs_1_), channel_id=1, source_target_pairs={{0,1},{1,0},{2,3},{3,2},{4,5},{5,4},{6,7},{7,6},{8,9},{9,8},{10,11... | collective-permute-start | bytes 786440 | tf_op jit(solution)/shard_map/ppermute | solution.py:453
  24.7 21.3 %copy-start.14 = (bf16[256,512]{1,0:T(8,128)(2,1)}, bf16[256,512]{1,0:T(8,128)(2,1)S(1)}, u32[]{:S(2)}) copy-start(bf16[256,512]{1,0:T(8,128)(2,1)S(1)} %collective-permute-done.4.refs_2_.refs_3_) | copy-start | bytes 786436
  24.7 16.5 %collective-permute-start.5 = (bf16[256,512]{1,0:T(8,128)(2,1)S(1)}, bf16[256,512]{1,0:T(8,128)(2,1)S(1)}, u32[]{:S(2)}, u32[]{:S(2)}) collective-permute-start(bf16[256,512]{1,0:T(8,128)(2,1)S(1)} %collective-permute-done.4.refs_2_.refs_3_), channel_id=1, source_target_pairs={{0,1},{1,0},{2,3},{3,2},{4,5},{5,4},{6,7},{7,6},{8,9},{9,8},{10,11... | collective-permute-start | bytes 786440 | tf_op jit(solution)/shard_map/ppermute | solution.py:453
  29.8 16.3 %copy-start.16 = (bf16[256,512]{1,0:T(8,128)(2,1)}, bf16[256,512]{1,0:T(8,128)(2,1)S(1)}, u32[]{:S(2)}) copy-start(bf16[256,512]{1,0:T(8,128)(2,1)S(1)} %collective-permute-done.6.refs_4_.refs_5_) | copy-start | bytes 786436
  29.8 11.5 %collective-permute-start.7 = (bf16[256,512]{1,0:T(8,128)(2,1)S(1)}, bf16[256,512]{1,0:T(8,128)(2,1)S(1)}, u32[]{:S(2)}, u32[]{:S(2)}) collective-permute-start(bf16[256,512]{1,0:T(8,128)(2,1)S(1)} %collective-permute-done.6.refs_4_.refs_5_), channel_id=1, source_target_pairs={{0,1},{1,0},{2,3},{3,2},{4,5},{5,4},{6,7},{7,6},{8,9},{9,8},{10,11... | collective-permute-start | bytes 786440 | tf_op jit(solution)/shard_map/ppermute | solution.py:453
  29.8 16.3 %copy-start.18 = (bf16[256,512]{1,0:T(8,128)(2,1)}, bf16[256,512]{1,0:T(8,128)(2,1)S(1)}, u32[]{:S(2)}) copy-start(bf16[256,512]{1,0:T(8,128)(2,1)S(1)} %collective-permute-done.8.refs_6_.refs_7_) | copy-start | bytes 786436
  29.8 11.5 %collective-permute-start.9 = (bf16[256,512]{1,0:T(8,128)(2,1)S(1)}, bf16[256,512]{1,0:T(8,128)(2,1)S(1)}, u32[]{:S(2)}, u32[]{:S(2)}) collective-permute-start(bf16[256,512]{1,0:T(8,128)(2,1)S(1)} %collective-permute-done.8.refs_6_.refs_7_), channel_id=1, source_target_pairs={{0,1},{1,0},{2,3},{3,2},{4,5},{5,4},{6,7},{7,6},{8,9},{9,8},{10,11... | collective-permute-start | bytes 786440 | tf_op jit(solution)/shard_map/ppermute | solution.py:453
  33.7 4.1 %copy-start.6 = (bf16[1024,4096]{1,0:T(8,128)(2,1)S(1)}, bf16[1024,4096]{1,0:T(8,128)(2,1)}, u32[]{:S(2)}) copy-start(bf16[1024,4096]{1,0:T(8,128)(2,1)} %refs_4_.15) | copy-start | bytes 25165828
  41.2 4.8 %copy-start.20 = (bf16[256,512]{1,0:T(8,128)(2,1)}, bf16[256,512]{1,0:T(8,128)(2,1)S(1)}, u32[]{:S(2)}) copy-start(bf16[256,512]{1,0:T(8,128)(2,1)S(1)} %collective-permute-done.3.refs_1_.refs_2_) | copy-start | bytes 786436
  41.3 4.8 %copy-start.22 = (bf16[256,512]{1,0:T(8,128)(2,1)}, bf16[256,512]{1,0:T(8,128)(2,1)S(1)}, u32[]{:S(2)}) copy-start(bf16[256,512]{1,0:T(8,128)(2,1)S(1)} %collective-permute-done.5.refs_3_.refs_4_) | copy-start | bytes 786436
  41.3 4.8 %copy-start.24 = (bf16[256,512]{1,0:T(8,128)(2,1)}, bf16[256,512]{1,0:T(8,128)(2,1)S(1)}, u32[]{:S(2)}) copy-start(bf16[256,512]{1,0:T(8,128)(2,1)S(1)} %collective-permute-done.7.refs_5_.refs_6_) | copy-start | bytes 786436
  41.3 4.8 %copy-start.26 = (bf16[256,512]{1,0:T(8,128)(2,1)}, bf16[256,512]{1,0:T(8,128)(2,1)S(1)}, u32[]{:S(2)}) copy-start(bf16[256,512]{1,0:T(8,128)(2,1)S(1)} %collective-permute-done.9.refs_7_.refs_8_) | copy-start | bytes 786436
  46.0 4.0 %copy-start.9 = (f32[4,128,512]{2,1,0:T(8,128)}, f32[4,128,512]{2,1,0:T(8,128)S(1)}, u32[]{:S(2)}) copy-start(f32[4,128,512]{2,1,0:T(8,128)S(1)} %get-tuple-element.41.mixed_ref) | copy-start | bytes 3145732
  50.0 2.0 %collective-permute-start.10 = (bf16[4,128,512]{2,1,0:T(8,128)(2,1)S(1)}, bf16[4,128,512]{2,1,0:T(8,128)(2,1)S(1)}, u32[]{:S(2)}, u32[]{:S(2)}) collective-permute-start(bf16[4,128,512]{2,1,0:T(8,128)(2,1)S(1)} %get-tuple-element.44), channel_id=1, source_target_pairs={{0,1},{1,0},{2,3},{3,2},{4,5},{5,4},{6,7},{7,6},{8,9},{9,8},{10,11... | collective-permute-start | bytes 1572872 | tf_op jit(solution)/shard_map/ppermute | solution.py:453
  52.7 16.8 %collective-permute-start.11 = (bf16[128,512]{1,0:T(8,128)(2,1)S(1)}, bf16[128,512]{1,0:T(8,128)(2,1)S(1)}, u32[]{:S(2)}, u32[]{:S(2)}) collective-permute-start(bf16[128,512]{1,0:T(8,128)(2,1)S(1)} %get-tuple-element.46), channel_id=1, source_target_pairs={{0,2},{1,3},{2,0},{3,1},{4,6},{5,7},{6,4},{7,5},{8,10},{9,11},{10,... | collective-permute-start | bytes 393224 | tf_op jit(solution)/shard_map/ppermute | solution.py:453
  63.1 13.4 %collective-permute-start.17 = (bf16[128,1024]{1,0:T(8,128)(2,1)}, bf16[128,1024]{1,0:T(8,128)(2,1)}, u32[]{:S(2)}, u32[]{:S(2)}) collective-permute-start(bf16[128,1024]{1,0:T(8,128)(2,1)} %get-tuple-element.51.refs_0_), channel_id=1, source_target_pairs={{0,8},{8,0},{16,24},{24,16},{1,9},{9,1},{17,25},{25,17},{2,10},{10... | collective-permute-start | bytes 786440 | tf_op jit(solution)/shard_map/ppermute | solution.py:453
  63.6 21.7 %collective-permute-start.18 = (bf16[128,1024]{1,0:T(8,128)(2,1)}, bf16[128,1024]{1,0:T(8,128)(2,1)}, u32[]{:S(2)}, u32[]{:S(2)}) collective-permute-start(bf16[128,1024]{1,0:T(8,128)(2,1)} %get-tuple-element.51.refs_0_), channel_id=1, source_target_pairs={{0,16},{8,24},{16,0},{24,8},{1,17},{9,25},{17,1},{25,9},{2,18},{10... | collective-permute-start | bytes 786440 | tf_op jit(solution)/shard_map/ppermute | solution.py:453
  64.7 20.6 %collective-permute-start.19 = (bf16[128,1024]{1,0:T(8,128)(2,1)}, bf16[128,1024]{1,0:T(8,128)(2,1)}, u32[]{:S(2)}, u32[]{:S(2)}) collective-permute-start(bf16[128,1024]{1,0:T(8,128)(2,1)} %get-tuple-element.51.refs_0_), channel_id=1, source_target_pairs={{0,24},{8,16},{16,8},{24,0},{1,25},{9,17},{17,9},{25,1},{2,26},{10... | collective-permute-start | bytes 786440 | tf_op jit(solution)/shard_map/ppermute | solution.py:453
  67.5 8.0 %collective-permute-start.12 = (bf16[128,512]{1,0:T(8,128)(2,1)}, bf16[128,512]{1,0:T(8,128)(2,1)S(1)}, u32[]{:S(2)}, u32[]{:S(2)}) collective-permute-start(bf16[128,512]{1,0:T(8,128)(2,1)} %get-tuple-element.47), channel_id=1, source_target_pairs={{0,4},{1,5},{2,6},{3,7},{4,0},{5,1},{6,2},{7,3},{8,12},{9,13},{10,... | collective-permute-start | bytes 393224 | tf_op jit(solution)/shard_map/ppermute | solution.py:453
  69.5 6.0 %collective-permute-start.13 = (bf16[128,512]{1,0:T(8,128)(2,1)S(1)}, bf16[128,512]{1,0:T(8,128)(2,1)S(1)}, u32[]{:S(2)}, u32[]{:S(2)}) collective-permute-start(bf16[128,512]{1,0:T(8,128)(2,1)S(1)} %get-tuple-element.48), channel_id=1, source_target_pairs={{0,6},{1,7},{2,4},{3,5},{4,2},{5,3},{6,0},{7,1},{8,14},{9,15},{10,... | collective-permute-start | bytes 393224 | tf_op jit(solution)/shard_map/ppermute | solution.py:453
  75.7 17.7 %copy-start.10 = (f32[4,128,512]{2,1,0:T(8,128)S(1)}, f32[4,128,512]{2,1,0:T(8,128)}, u32[]{:S(2)}) copy-start(f32[4,128,512]{2,1,0:T(8,128)} %copy-done.9) | copy-start | bytes 3145732
  75.7 17.7 %copy-start.12 = (bf16[256,512]{1,0:T(8,128)(2,1)S(1)}, bf16[256,512]{1,0:T(8,128)(2,1)}, u32[]{:S(2)}) copy-start(bf16[256,512]{1,0:T(8,128)(2,1)} %copy-done.11) | copy-start | bytes 786436
  75.7 20.9 %slice-start = ((s8[8388608]{0:T(1024)(128)(4,1)}), s8[4194304]{0:T(1024)(128)(4,1)S(1)}, s32[]{:S(2)}) async-start(s8[8388608]{0:T(1024)(128)(4,1)} %bitcast.1), calls=%async_computation | async-start | bytes 8388608
  76.5 20.2 %slice-start.1 = ((s8[8388608]{0:T(1024)(128)(4,1)}), s8[4194304]{0:T(1024)(128)(4,1)S(1)}, s32[]{:S(2)}) async-start(s8[8388608]{0:T(1024)(128)(4,1)} %bitcast.1), calls=%async_computation.1 | async-start | bytes 8388608
  88.6 4.8 %copy-start.15 = (bf16[256,512]{1,0:T(8,128)(2,1)S(1)}, bf16[256,512]{1,0:T(8,128)(2,1)}, u32[]{:S(2)}) copy-start(bf16[256,512]{1,0:T(8,128)(2,1)} %copy-done.14) | copy-start | bytes 786436
  88.6 4.8 %copy-start.17 = (bf16[256,512]{1,0:T(8,128)(2,1)S(1)}, bf16[256,512]{1,0:T(8,128)(2,1)}, u32[]{:S(2)}) copy-start(bf16[256,512]{1,0:T(8,128)(2,1)} %copy-done.16) | copy-start | bytes 786436
  88.6 4.8 %copy-start.19 = (bf16[256,512]{1,0:T(8,128)(2,1)S(1)}, bf16[256,512]{1,0:T(8,128)(2,1)}, u32[]{:S(2)}) copy-start(bf16[256,512]{1,0:T(8,128)(2,1)} %copy-done.18) | copy-start | bytes 786436
  88.6 4.8 %copy-start.21 = (bf16[256,512]{1,0:T(8,128)(2,1)S(1)}, bf16[256,512]{1,0:T(8,128)(2,1)}, u32[]{:S(2)}) copy-start(bf16[256,512]{1,0:T(8,128)(2,1)} %copy-done.20) | copy-start | bytes 786436
  88.6 4.8 %copy-start.23 = (bf16[256,512]{1,0:T(8,128)(2,1)S(1)}, bf16[256,512]{1,0:T(8,128)(2,1)}, u32[]{:S(2)}) copy-start(bf16[256,512]{1,0:T(8,128)(2,1)} %copy-done.22) | copy-start | bytes 786436
  88.7 4.8 %copy-start.25 = (bf16[256,512]{1,0:T(8,128)(2,1)S(1)}, bf16[256,512]{1,0:T(8,128)(2,1)}, u32[]{:S(2)}) copy-start(bf16[256,512]{1,0:T(8,128)(2,1)} %copy-done.24) | copy-start | bytes 786436
  88.7 4.8 %copy-start.27 = (bf16[256,512]{1,0:T(8,128)(2,1)S(1)}, bf16[256,512]{1,0:T(8,128)(2,1)}, u32[]{:S(2)}) copy-start(bf16[256,512]{1,0:T(8,128)(2,1)} %copy-done.26) | copy-start | bytes 786436
  96.5 3.7 %collective-permute-start.20 = (bf16[4,128,512]{2,1,0:T(8,128)(2,1)S(1)}, bf16[4,128,512]{2,1,0:T(8,128)(2,1)S(1)}, u32[]{:S(2)}, u32[]{:S(2)}) collective-permute-start(bf16[4,128,512]{2,1,0:T(8,128)(2,1)S(1)} %get-tuple-element.58), channel_id=1, source_target_pairs={{0,1},{1,0},{2,3},{3,2},{4,5},{5,4},{6,7},{7,6},{8,9},{9,8},{10,11... | collective-permute-start | bytes 1572872 | tf_op jit(solution)/shard_map/ppermute | solution.py:453
  98.8 25.0 %collective-permute-start.16 = (bf16[128,1024]{1,0:T(8,128)(2,1)S(1)}, bf16[128,1024]{1,0:T(8,128)(2,1)S(1)}, u32[]{:S(2)}, u32[]{:S(2)}) collective-permute-start(bf16[128,1024]{1,0:T(8,128)(2,1)S(1)} %all_terms.10), channel_id=1, source_target_pairs={{0,24},{8,16},{16,8},{24,0},{1,25},{9,17},{17,9},{25,1},{2,26},{10... | collective-permute-start | bytes 786440 | tf_op jit(solution)/shard_map/ppermute | solution.py:453
  100.4 17.4 %collective-permute-start.21 = (bf16[128,512]{1,0:T(8,128)(2,1)S(1)}, bf16[128,512]{1,0:T(8,128)(2,1)S(1)}, u32[]{:S(2)}, u32[]{:S(2)}) collective-permute-start(bf16[128,512]{1,0:T(8,128)(2,1)S(1)} %get-tuple-element.60), channel_id=1, source_target_pairs={{0,2},{1,3},{2,0},{3,1},{4,6},{5,7},{6,4},{7,5},{8,10},{9,11},{10,... | collective-permute-start | bytes 393224 | tf_op jit(solution)/shard_map/ppermute | solution.py:453
  102.7 15.1 %collective-permute-start.22 = (bf16[128,512]{1,0:T(8,128)(2,1)S(1)}, bf16[128,512]{1,0:T(8,128)(2,1)S(1)}, u32[]{:S(2)}, u32[]{:S(2)}) collective-permute-start(bf16[128,512]{1,0:T(8,128)(2,1)S(1)} %get-tuple-element.61), channel_id=1, source_target_pairs={{0,4},{1,5},{2,6},{3,7},{4,0},{5,1},{6,2},{7,3},{8,12},{9,13},{10,... | collective-permute-start | bytes 393224 | tf_op jit(solution)/shard_map/ppermute | solution.py:453
  103.9 13.9 %collective-permute-start.23 = (bf16[128,512]{1,0:T(8,128)(2,1)S(1)}, bf16[128,512]{1,0:T(8,128)(2,1)S(1)}, u32[]{:S(2)}, u32[]{:S(2)}) collective-permute-start(bf16[128,512]{1,0:T(8,128)(2,1)S(1)} %get-tuple-element.62), channel_id=1, source_target_pairs={{0,6},{1,7},{2,4},{3,5},{4,2},{5,3},{6,0},{7,1},{8,14},{9,15},{10,... | collective-permute-start | bytes 393224 | tf_op jit(solution)/shard_map/ppermute | solution.py:453
  107.7 29.5 %collective-permute-start.15 = (bf16[128,1024]{1,0:T(8,128)(2,1)S(1)}, bf16[128,1024]{1,0:T(8,128)(2,1)S(1)}, u32[]{:S(2)}, u32[]{:S(2)}) collective-permute-start(bf16[128,1024]{1,0:T(8,128)(2,1)S(1)} %all_terms.9), channel_id=1, source_target_pairs={{0,16},{8,24},{16,0},{24,8},{1,17},{9,25},{17,1},{25,9},{2,18},{10... | collective-permute-start | bytes 786440 | tf_op jit(solution)/shard_map/ppermute | solution.py:453
  117.8 19.8 %collective-permute-start.14 = (bf16[128,1024]{1,0:T(8,128)(2,1)S(1)}, bf16[128,1024]{1,0:T(8,128)(2,1)S(1)}, u32[]{:S(2)}, u32[]{:S(2)}) collective-permute-start(bf16[128,1024]{1,0:T(8,128)(2,1)S(1)} %all_terms.8), channel_id=1, source_target_pairs={{0,8},{8,0},{16,24},{24,16},{1,9},{9,1},{17,25},{25,17},{2,10},{10... | collective-permute-start | bytes 786440 | tf_op jit(solution)/shard_map/ppermute | solution.py:453
  118.7 18.9 %collective-permute-start.26 = (bf16[128,1024]{1,0:T(8,128)(2,1)S(1)}, bf16[128,1024]{1,0:T(8,128)(2,1)S(1)}, u32[]{:S(2)}, u32[]{:S(2)}) collective-permute-start(bf16[128,1024]{1,0:T(8,128)(2,1)S(1)} %all_terms.14), channel_id=1, source_target_pairs={{0,24},{8,16},{16,8},{24,0},{1,25},{9,17},{17,9},{25,1},{2,26},{10... | collective-permute-start | bytes 786440 | tf_op jit(solution)/shard_map/ppermute | solution.py:453
  121.0 27.7 %collective-permute-start.25 = (bf16[128,1024]{1,0:T(8,128)(2,1)S(1)}, bf16[128,1024]{1,0:T(8,128)(2,1)S(1)}, u32[]{:S(2)}, u32[]{:S(2)}) collective-permute-start(bf16[128,1024]{1,0:T(8,128)(2,1)S(1)} %all_terms.13), channel_id=1, source_target_pairs={{0,16},{8,24},{16,0},{24,8},{1,17},{9,25},{17,1},{25,9},{2,18},{10... | collective-permute-start | bytes 786440 | tf_op jit(solution)/shard_map/ppermute | solution.py:453
  123.8 24.9 %collective-permute-start.24 = (bf16[128,1024]{1,0:T(8,128)(2,1)S(1)}, bf16[128,1024]{1,0:T(8,128)(2,1)S(1)}, u32[]{:S(2)}, u32[]{:S(2)}) collective-permute-start(bf16[128,1024]{1,0:T(8,128)(2,1)S(1)} %all_terms.12), channel_id=1, source_target_pairs={{0,8},{8,0},{16,24},{24,16},{1,9},{9,1},{17,25},{25,17},{2,10},{10... | collective-permute-start | bytes 786440 | tf_op jit(solution)/shard_map/ppermute | solution.py:453
  (12 other events, 27.9 us)
